TPU v7x, 128 devices: a whole 4x4x4 slice. The times are simulated.
128 devices in a mesh: dp: 4 (over y), graph: 32 (over z, x, core).
Axes of the slice: x: 4, y: 4, z: 4, core: 2. Of those that a mesh axis runs over, the one named last changes fastest.
Arguments:
- messages: bfloat16 [4, 32768, 512], P('dp', 'graph'), may hold values from -6 to 6
- cotangent: bfloat16 [4, 32768, 512], P('dp', 'graph'), may hold values from -6 to 6
- triplet_basis: bfloat16 [4, 32768, 3584], P('dp', 'graph'), may hold values from -6 to 6
- w_edge: bfloat16 [512, 512], replicated, may hold values from -0.25 to 0.25
- w_down: bfloat16 [512, 64], replicated, may hold values from -0.25 to 0.25
- w_bil: bfloat16 [112, 4096], replicated, may hold values from -0.01171875 to 0.01171875
- w_up: bfloat16 [2, 64, 512], replicated, may hold values from -0.75 to 0.75
- trip_src: int32 [4, 32768, 32], P('dp', 'graph'), may hold values from -1 to 2047, as said below
- send_rows: int32 [4, 128, 256], P('dp', 'graph'), may hold values from 0 to 1023, as said below
- send_count: int32 [4, 128], P('dp', 'graph'), may hold values from 1 to 256, as said below
- rev_src: int32 [4, 32768], P('dp', 'graph'), may hold values from -1 to 2047, as said below
- edge_count: int32 [4, 32], P('dp', 'graph'), may hold values from 614 to 1024, as said below
Outputs:
- grad_messages: bfloat16 [4, 32768, 512], P('dp', 'graph')
- grad_w_edge: float32 [512, 512], P('graph')
- grad_w_down: float32 [512, 64], P('graph')
- grad_w_bil: float32 [112, 4096], P(None, 'graph')
- grad_w_up: float32 [2, 64, 512], P(None, None, 'graph')
Inputs may be any that keep to these rules, and one draw needn't show every extreme that they name: `trip_src`: an entry below 1024 is a live edge of the same device; an entry 1024 + o * 256 + c names row c, below its count, of send list o of the device off(o) positions lower along graph (cyclically). Slots k at or beyond an edge's triplet count, and all slots of empty edges, are -1. `send_rows`: send list o of a device goes to the device off(o) positions higher along graph, cyclically. Its entries are distinct live rows; entries at or beyond the list's count are padding. `send_count`: in each slab some list holds exactly 256 rows. `rev_src`: every live edge has one reverse edge, on its own device or within 2 devices; if edge e reads row r as its reverse, the edge behind r reads e back. Empty slots hold -1. `edge_count`: in each slab some device is full.
All inputs are finite; a program needn't handle non-finite values.
Results may differ from a plain program's by a relative error of at most 0.023.
Values may be sent and summed in bfloat16 or wider, within the bound.
A program may use at most 192 MiB of HBM per device.

v0:
```python
import math

import jax
import jax.numpy as jnp
from jax import lax
from jax.sharding import PartitionSpec as P

inv_root = 0.7071067811865476


def shifted(block, axis, distance):
    devices = range(lax.axis_size(axis))
    route = [((i - distance) % len(devices), i) for i in devices]
    return lax.ppermute(block, axis, route)


def silu_slope(values):
    sigma = jax.nn.sigmoid(values)
    return sigma * (1.0 + values * (1.0 - sigma))


def offsets(count):
    return [(which // 2 + 1) * (1 - 2 * (which % 2)) for which in range(count)]


def contract(left, right):
    return lax.dot_general(
        left, right, (((0,), (0,)), ((), ())), preferred_element_type=jnp.float32
    )


def packed(members, list_count):
    return jnp.concatenate([member.reshape(list_count, -1, 128) for member in members], axis=1)


def unpacked(bundle, widths, list_count, slot_count):
    pieces = []
    offset_row = 0
    for columns in widths:
        extent = slot_count * columns // 128
        pieces.append(
            bundle[:, offset_row : offset_row + extent].reshape(list_count, slot_count, columns)
        )
        offset_row = offset_row + extent
    return pieces


def deliver(payload, direction):
    list_count = payload.shape[0]
    shifts = offsets(list_count)
    arrived = []
    for which in range(list_count):
        arrived.append(shifted(payload[which], "graph", direction * shifts[which]))
    return jnp.stack(arrived)


def body(
    messages,
    cotangent,
    triplet_basis,
    w_edge,
    w_down,
    w_bil,
    w_up,
    trip_src,
    send_rows,
    send_count,
    rev_src,
    edge_count,
):
    edges = messages.shape[1]
    model = messages.shape[2]
    narrow = w_down.shape[1]
    slots = trip_src.shape[2]
    capacity = send_rows.shape[2]
    list_count = send_rows.shape[1]
    basis_count = w_bil.shape[0]
    pool_size = edges + list_count * capacity
    source = messages[0]
    own_cot = cotangent[0]
    alive = jnp.arange(edges) < edge_count[0, 0]
    pre_edge = jnp.dot(source, w_edge, preferred_element_type=jnp.float32)
    hidden = jax.nn.silu(pre_edge).astype(jnp.bfloat16)
    pre_down = jnp.dot(hidden, w_down, preferred_element_type=jnp.float32)
    reduced = jax.nn.silu(pre_down).astype(jnp.bfloat16)
    list_rows = send_rows[0]
    filled = jnp.arange(capacity)[None, :] < send_count[0][:, None]

    def outgoing(values):
        picked = values[list_rows]
        return jnp.where(filled[:, :, None], picked, jnp.zeros((), values.dtype))

    scaled = jnp.where(alive[:, None], own_cot.astype(jnp.float32) * inv_root, 0.0)
    arrived = deliver(packed([outgoing(reduced), outgoing(own_cot)], list_count), 1)
    recv_red, recv_cot = unpacked(arrived, [narrow, model], list_count, capacity)
    pool_cot = jnp.concatenate([own_cot, recv_cot.reshape(-1, model)], axis=0)
    pool_red = jnp.concatenate([reduced, recv_red.reshape(-1, narrow)], axis=0)
    trips = trip_src[0]
    valid = trips >= 0
    trip_index = jnp.maximum(trips, 0)
    gathered = jnp.where(valid[:, :, None], pool_red[trip_index], jnp.zeros((), jnp.bfloat16))
    basis = triplet_basis[0].reshape(edges, slots, basis_count)
    outer = jnp.einsum("ekb,ekc->ebc", basis, gathered, preferred_element_type=jnp.float32)
    outer = outer.astype(jnp.bfloat16).reshape(edges, basis_count * narrow)
    w_flat = w_bil.reshape(basis_count * narrow, narrow)
    state = jnp.dot(outer, w_flat, preferred_element_type=jnp.float32).astype(jnp.bfloat16)
    pre_ca = jnp.dot(state, w_up[0], preferred_element_type=jnp.float32)
    grad_ca = (scaled * silu_slope(pre_ca)).astype(jnp.bfloat16)
    up_ca = contract(state, grad_ca)
    grad_own = jnp.dot(grad_ca, w_up[0].T, preferred_element_type=jnp.float32)
    reverse = rev_src[0]
    has_rev = reverse >= 0
    rev_index = jnp.maximum(reverse, 0)
    mirror = jnp.where(has_rev[:, None], pool_cot[rev_index], jnp.zeros((), jnp.bfloat16))
    pre_ac = jnp.dot(state, w_up[1], preferred_element_type=jnp.float32)
    grad_ac = (mirror.astype(jnp.float32) * inv_root * silu_slope(pre_ac)).astype(jnp.bfloat16)
    up_ac = contract(state, grad_ac)
    back_rev = jnp.dot(grad_ac, w_up[1].T, preferred_element_type=jnp.float32).astype(jnp.bfloat16)
    grad_state = (grad_own + back_rev.astype(jnp.float32)).astype(jnp.bfloat16)
    grad_outer = jnp.dot(grad_state, w_flat.T, preferred_element_type=jnp.float32).astype(
        jnp.bfloat16
    )
    bil = contract(outer, grad_state)
    grad_trip = jnp.einsum(
        "ebc,ekb->ekc",
        grad_outer.reshape(edges, basis_count, narrow),
        basis,
        preferred_element_type=jnp.float32,
    )
    grad_trip = jnp.where(valid[:, :, None], grad_trip, 0.0)
    grad_pool = (
        jnp.zeros((pool_size, narrow), jnp.float32)
        .at[trip_index.reshape(-1)]
        .add(grad_trip.reshape(-1, narrow))
    )
    grad_send = grad_pool[edges:].astype(jnp.bfloat16).reshape(list_count, capacity, narrow)
    grad_arrived = deliver(packed([grad_send], list_count), -1)
    (grad_back,) = unpacked(grad_arrived, [narrow], list_count, capacity)
    grad_red = (
        grad_pool[:edges]
        .at[list_rows.reshape(-1)]
        .add(jnp.where(filled[:, :, None], grad_back.astype(jnp.float32), 0.0).reshape(-1, narrow))
    )
    grad_down = (grad_red * silu_slope(pre_down)).astype(jnp.bfloat16)
    down_sum = contract(hidden, grad_down)
    grad_hidden = jnp.dot(grad_down, w_down.T, preferred_element_type=jnp.float32)
    grad_edge = (grad_hidden * silu_slope(pre_edge)).astype(jnp.bfloat16)
    edge_sum = contract(source, grad_edge)
    grad_messages = jnp.dot(grad_edge, w_edge.T, preferred_element_type=jnp.float32).astype(
        jnp.bfloat16
    )[None]
    factor = 1.0 / math.sqrt(lax.axis_size("dp") * lax.axis_size("graph") * edges)
    shares = (
        lax.psum_scatter(
            (edge_sum * factor).astype(jnp.bfloat16), "graph", scatter_dimension=0, tiled=True
        ).astype(jnp.float32),
        lax.psum_scatter(
            (down_sum * factor).astype(jnp.bfloat16), "graph", scatter_dimension=0, tiled=True
        ).astype(jnp.float32),
        lax.psum_scatter(
            (bil.reshape(basis_count, narrow * narrow) * factor).astype(jnp.bfloat16),
            "graph",
            scatter_dimension=1,
            tiled=True,
        ).astype(jnp.float32),
        lax.psum_scatter(
            (jnp.stack([up_ca, up_ac]) * factor).astype(jnp.bfloat16),
            "graph",
            scatter_dimension=2,
            tiled=True,
        ).astype(jnp.float32),
    )
    totals = (
        lax.psum(shares[0].astype(jnp.bfloat16), "dp").astype(jnp.float32),
        lax.psum(shares[1].astype(jnp.bfloat16), "dp").astype(jnp.float32),
        lax.psum(shares[2].astype(jnp.bfloat16), "dp").astype(jnp.float32),
        lax.psum(shares[3].astype(jnp.bfloat16), "dp").astype(jnp.float32),
    )
    return (grad_messages, totals[0], totals[1], totals[2], totals[3])


def solution(mesh):
    return jax.shard_map(
        body,
        mesh=mesh,
        in_specs=(
            P("dp", "graph", None),
            P("dp", "graph", None),
            P("dp", "graph", None),
            P(),
            P(),
            P(),
            P(),
            P("dp", "graph", None),
            P("dp", "graph", None),
            P("dp", "graph"),
            P("dp", "graph"),
            P("dp", "graph"),
        ),
        out_specs=(
            P("dp", "graph", None),
            P("graph", None),
            P("graph", None),
            P(None, "graph"),
            P(None, None, "graph"),
        ),
        check_vma=False,
    )
```

profile of v0, /device:TPU:0, one launch (start us, length us, event | category | flops | bytes accessed | tf_op | source)
XLA Modules:
  0.0 894.0 jit_solution(11844233610408868876)
XLA Ops:
  7.2 1.2 copy-done
  8.4 3.3 multiply_convert_fusion.3
  11.7 1.2 multiply_convert_fusion.5
  13.2 3.2 gather_fusion
  16.8 4.0 gather_fusion.1
  20.7 1.4 gather.16
  22.4 0.3 broadcast_in_dim.116
  22.8 2.7 broadcast_select_fusion
  25.5 1.1 fusion.19
  26.6 5.8 collective-permute-start.1
  32.3 5.3 collective-permute-start.3
  38.2 10.4 %copy.47 = bf16[1,1024,3584]{1,2,0:T(8,128)(2,1)} copy(bf16[1,1024,3584]{2,1,0:T(8,128)(2,1)} %param.14) | data formatting | bytes 14680064 | tf_op args[2]
  48.6 12.2 %copy.48 = bf16[1024,32,112]{2,1,0:T(8,128)(2,1)} copy(bf16[1024,32,112]{0,2,1:T(8,128)(2,1)} %bitcast.104) | data formatting | bytes 14680064 | tf_op jit(solution)/shard_map/reshape;squeeze | solution.py:102
  61.1 3.8 reshape.197
  65.5 0.6 iota_compare_fusion.1
  66.1 0.8 pad_maximum_fusion.7
  66.9 2.1 pad_maximum_fusion.1
  69.7 114.9 %gather_fusion.2 = bf16[32768,64]{1,0:T(8,128)(2,1)} fusion(bf16[2048,64]{1,0:T(8,128)(2,1)S(1)} %copy.46, s32[32768]{0:T(1024)S(1)} %broadcast_clamp_fusion), kind=kCustom, calls=%fused_computation.2 | custom fusion | bytes 8519680 | tf_op jit(solution)/shard_map/gather | solution.py:101
  184.6 16.3 %convert_bitcast_fusion = bf16[1024,112,64]{1,2,0:T(8,128)(2,1)} fusion(bf16[1024,32,112]{2,1,0:T(8,128)(2,1)} %copy.48, bf16[1024,32,64]{2,1,0:T(8,128)(2,1)} %bitcast.103, pred[1024,32]{1,0:T(8,128)(4,1)S(1)} %copy.42), kind=kOutput, calls=%fused_computation.6 | convolution fusion | flops 479199232 | bytes 26247168 | tf_op jit(solution)/shard_map/ekb,ekc->ebc/dot_general | solution.py:103
  200.9 25.6 %copy.49 = bf16[1024,112,64]{0,2,1:T(8,128)(2,1)} copy(bf16[1024,112,64]{1,2,0:T(8,128)(2,1)} %convert_bitcast_fusion) | data formatting | bytes 29360128 | tf_op jit(solution)/shard_map/convert_element_type | solution.py:104
  226.5 1.4 reshape_reshape.8
  228.0 2.8 pad_maximum_fusion
  230.8 8.0 convolution_convert_fusion.3
  238.8 5.9 gather_fusion.3
  244.6 2.0 multiply_convert_fusion.1
  246.6 0.4 fusion.7
  247.1 0.3 convolution_bitcast_fusion
  247.4 1.1 multiply_convert_fusion.2
  248.8 0.4 fusion.8
  249.2 0.8 copy-done.3
  250.0 7.4 convolution_convert_fusion
  257.3 20.0 %copy.50 = bf16[1024,7168]{0,1:T(8,128)(2,1)} copy(bf16[1024,7168]{1,0:T(8,128)(2,1)} %convolution_convert_fusion) | data formatting | bytes 29360128 | tf_op jit(solution)/shard_map/convert_element_type | solution.py:120
  277.3 25.2 %copy.51 = bf16[1024,112,64]{1,2,0:T(8,128)(2,1)} copy(bf16[1024,112,64]{0,2,1:T(8,128)(2,1)} %bitcast.102) | data formatting | bytes 29360128 | tf_op jit(solution)/shard_map/reshape | solution.py:126
  302.5 20.1 %convolution_select_fusion = f32[1024,64,32]{1,2,0:T(8,128)} fusion(bf16[1024,112,64]{1,2,0:T(8,128)(2,1)} %copy.51, bf16[1024,32,112]{2,1,0:T(8,128)(2,1)} %copy.48, pred[1024,32]{1,0:T(8,128)(4,1)S(1)} %copy.42), kind=kOutput, calls=%fused_computation.8 | convolution fusion | flops 471859200 | bytes 30441472 | tf_op jit(solution)/shard_map/ebc,ekb->ekc/dot_general | solution.py:124
  322.6 186.5 %scatter_custom_fusion = f32[2048,64]{1,0:T(8,128)S(1)} fusion(s32[32768]{0:T(1024)S(1)} %reshape.235, f32[32768,64]{1,0:T(8,128)} %bitcast.105, f32[]{:T(128)} %constant.7.clone.1), kind=kCustom, calls=%fused_computation.49 | custom fusion | flops 2097152 | bytes 524800 | tf_op jit(solution)/shard_map/scatter-add | solution.py:134
  509.3 12.8 %collective-permute-start.4 = (bf16[128,128]{1,0:T(8,128)(2,1)S(1)}, bf16[128,128]{1,0:T(8,128)(2,1)S(1)}, u32[]{:S(2)}, u32[]{:S(2)}) collective-permute-start(bf16[128,128]{1,0:T(8,128)(2,1)S(1)} %squeeze.56), channel_id=1, source_target_pairs={{1,0},{2,1},{3,2},{4,3},{5,4},{6,5},{7,6},{8,7},{9,8},{10,9},{11,1... | collective-permute-start | bytes 98312 | tf_op jit(solution)/shard_map/ppermute | solution.py:14
  522.4 0.5 collective-permute-start.6
  522.9 1.7 collective-permute-start.7
  524.7 0.9 copy.55
  525.8 3.1 collective-permute-done.5
  529.1 1.1 collective-permute-done.7
  530.4 7.1 scatter_custom_fusion.1
  537.8 2.5 multiply_convert_fusion
  540.3 0.7 fusion.6
  541.3 1.1 copy.58
  542.4 10.7 %fusion.2 = bf16[7168,64]{0,1:T(8,128)(2,1)} fusion(bf16[1024,7168]{0,1:T(8,128)(2,1)} %bitcast.101, bf16[1024,64]{0,1:T(8,128)(2,1)S(1)} %fusion.8), kind=kOutput, calls=%fused_computation.12 | convolution fusion | flops 940441600 | bytes 15728640 | tf_op jit(solution)/shard_map/dot_general | solution.py:27
  553.2 1.9 copy.54
  555.1 2.3 convert_element_type.118
  557.3 2.3 copy.60
  559.7 0.6 dynamic-slice
  561.0 2.9 fusion.4
  563.9 1.1 fusion.9
  565.1 63.4 %all-reduce.4.cloned.1.call-done = bf16[2,64,512]{1,0,2:T(2,128)(2,1)} async-done(((bf16[2,64,512]{1,0,2:T(2,128)(2,1)}), bf16[2,64,512]{1,0,2:T(2,128)(2,1)}) %all-reduce.4.cloned.1.call-update) | async-done | bytes 131088
  628.4 0.7 constant_dynamic-slice_fusion
  629.1 79.8 %reduce-scatter.10.cloned.1.call-done = bf16[16,512]{1,0:T(8,128)(2,1)} async-done(((bf16[512,512]{1,0:T(8,128)(2,1)}), bf16[16,512]{1,0:T(8,128)(2,1)}) %reduce-scatter.10.cloned.1.call-update) | async-done | bytes 16400
  708.9 0.8 copy.59
  709.8 79.9 %reduce-scatter.12.cloned.1.call-done = bf16[128,112]{1,0:T(8,128)(2,1)} async-done(((bf16[4096,112]{1,0:T(8,128)(2,1)}), bf16[128,112]{1,0:T(8,128)(2,1)}) %reduce-scatter.12.cloned.1.call-update) | async-done | bytes 28688
  789.7 0.9 copy.61
  790.6 75.0 %reduce-scatter.8.cloned.1.call-done = bf16[16,64]{1,0:T(8,128)(2,1)} async-done(((bf16[512,64]{1,0:T(8,128)(2,1)}), bf16[16,64]{1,0:T(8,128)(2,1)}) %reduce-scatter.8.cloned.1.call-update) | async-done | bytes 2064 | tf_op jit(solution)/shard_map/reduce_scatter | solution.py:157
  865.6 19.3 %all-reduce.1 = (bf16[16,512]{0,1:T(8,128)(2,1)S(1)}, bf16[2,64,16]{1,0,2:T(2,128)(2,1)S(1)}, bf16[16,64]{1,0:T(8,128)(2,1)S(1)}, bf16[112,128]{1,0:T(8,128)(2,1)S(1)}) all-reduce(bf16[16,512]{0,1:T(8,128)(2,1)S(1)} %copy.59, bf16[2,64,16]{1,0,2:T(2,128)(2,1)S(1)} %constant_dynamic-slice_fusion, ...), channel_id=1, replica_groups=mesh['dp'=4,'graph'=32] {'dp'}, use_global_device_ids=true, to_apply=%region_3.4 | all-reduce | flops 25600 | bytes 102400 | tf_op jit(solution)/shard_map/psum | solution.py:174
  884.9 0.6 convert_element_type.119
  885.6 0.7 copy.56
  886.3 0.6 copy.57
  886.9 0.6 convert_element_type.116
  (93 shorter events, 4.2 us)
Async XLA Ops:
  7.2 1.2 copy-start
  7.2 4.5 copy-start.11
  7.2 621.2 %all-reduce.4.cloned.1.call-start = ((), (), s32[]{:S(2)}) async-start(), calls=%async_computation.6 | async-start | bytes 524288
  11.7 1.2 copy-start.16
  11.7 1.4 copy-start.9
  11.7 1.4 copy-start.13
  12.9 3.9 copy-start.1
  22.7 14.9 %copy-start.5 = (s32[1,1024,32]{1,2,0:T(8,128)S(1)}, s32[1,1024,32]{1,2,0:T(8,128)}, u32[]{:S(2)}) copy-start(s32[1,1024,32]{1,2,0:T(8,128)} %param.19) | copy-start | bytes 393220
  22.7 15.0 %copy-start.8 = (s32[1,1024]{1,0:T(1,128)S(1)}, s32[1,1024]{1,0:T(1,128)}, u32[]{:S(2)}) copy-start(s32[1,1024]{1,0:T(1,128)} %param.22) | copy-start | bytes 12292
  26.6 39.5 %collective-permute-start.1 = (bf16[1152,128]{1,0:T(8,128)(2,1)}, bf16[1152,128]{1,0:T(8,128)(2,1)S(1)}, u32[]{:S(2)}, u32[]{:S(2)}) collective-permute-start(bf16[1152,128]{1,0:T(8,128)(2,1)} %get-tuple-element.25), channel_id=1, source_target_pairs={{1,0},{2,1},{3,2},{4,3},{5,4},{6,5},{7,6},{8,7},{9,8},{10,9},{11,1... | collective-permute-start | bytes 884744 | tf_op jit(solution)/shard_map/ppermute | solution.py:14
  32.3 33.8 %collective-permute-start.2 = (bf16[1152,128]{1,0:T(8,128)(2,1)}, bf16[1152,128]{1,0:T(8,128)(2,1)}, u32[]{:S(2)}, u32[]{:S(2)}) collective-permute-start(bf16[1152,128]{1,0:T(8,128)(2,1)} %get-tuple-element.27), channel_id=1, source_target_pairs={{30,0},{31,1},{0,2},{1,3},{2,4},{3,5},{4,6},{5,7},{6,8},{7,9},{8,1... | collective-permute-start | bytes 884744 | tf_op jit(solution)/shard_map/ppermute | solution.py:14
  32.3 33.8 %collective-permute-start.3 = (bf16[1152,128]{1,0:T(8,128)(2,1)}, bf16[1152,128]{1,0:T(8,128)(2,1)}, u32[]{:S(2)}, u32[]{:S(2)}) collective-permute-start(bf16[1152,128]{1,0:T(8,128)(2,1)} %get-tuple-element.26), channel_id=1, source_target_pairs={{2,0},{3,1},{4,2},{5,3},{6,4},{7,5},{8,6},{9,7},{10,8},{11,9},{12,... | collective-permute-start | bytes 884744 | tf_op jit(solution)/shard_map/ppermute | solution.py:14
  37.7 28.5 %collective-permute-start = (bf16[1152,128]{1,0:T(8,128)(2,1)}, bf16[1152,128]{1,0:T(8,128)(2,1)}, u32[]{:S(2)}, u32[]{:S(2)}) collective-permute-start(bf16[1152,128]{1,0:T(8,128)(2,1)} %get-tuple-element.24), channel_id=1, source_target_pairs={{31,0},{0,1},{1,2},{2,3},{3,4},{4,5},{5,6},{6,7},{7,8},{8,9},{9,10... | collective-permute-start | bytes 884744 | tf_op jit(solution)/shard_map/ppermute | solution.py:14
  200.9 25.6 %copy-start.4 = (bf16[4,1024,128]{2,1,0:T(8,128)(2,1)S(1)}, bf16[4,1024,128]{2,1,0:T(8,128)(2,1)}, u32[]{:S(2)}) copy-start(bf16[4,1024,128]{2,1,0:T(8,128)(2,1)} %pad_maximum_fusion.1) | copy-start | bytes 3145732
  227.9 2.8 copy-start.2
  244.6 2.0 copy-start.7
  246.6 0.8 copy-start.14
  248.5 1.5 copy-start.3
  509.3 16.4 %collective-permute-start.4 = (bf16[128,128]{1,0:T(8,128)(2,1)S(1)}, bf16[128,128]{1,0:T(8,128)(2,1)S(1)}, u32[]{:S(2)}, u32[]{:S(2)}) collective-permute-start(bf16[128,128]{1,0:T(8,128)(2,1)S(1)} %squeeze.56), channel_id=1, source_target_pairs={{1,0},{2,1},{3,2},{4,3},{5,4},{6,5},{7,6},{8,7},{9,8},{10,9},{11,1... | collective-permute-start | bytes 98312 | tf_op jit(solution)/shard_map/ppermute | solution.py:14
  522.2 6.7 collective-permute-start.5
  522.4 6.6 collective-permute-start.6
  522.9 7.3 collective-permute-start.7
  524.7 13.0 %copy-start.6 = (f32[1024,64]{0,1:T(8,128)S(1)}, f32[1024,64]{0,1:T(8,128)}, u32[]{:S(2)}) copy-start(f32[1024,64]{0,1:T(8,128)} %get-tuple-element.35) | copy-start | bytes 786436
  524.7 13.1 %copy-start.12 = (bf16[512,64]{0,1:T(8,128)(2,1)S(1)}, bf16[512,64]{0,1:T(8,128)(2,1)}, u32[]{:S(2)}) copy-start(bf16[512,64]{0,1:T(8,128)(2,1)} %param.16) | copy-start | bytes 196612
  525.6 183.3 %reduce-scatter.10.cloned.1.call-start = ((), (), s32[]{:S(2)}) async-start(), calls=%async_computation.4 | async-start | bytes 540672
  540.3 1.0 copy-start.18
  542.4 247.3 %reduce-scatter.12.cloned.1.call-start = ((), (), s32[]{:S(2)}) async-start(), calls=%async_computation.5 | async-start | bytes 1081344
  557.3 2.4 copy-start.15
  557.3 3.6 copy-start.10
  559.6 4.3 copy-start.17
  559.6 305.9 %reduce-scatter.8.cloned.1.call-start = ((), (), s32[]{:S(2)}) async-start(), calls=%async_computation.3 | async-start | bytes 135168 | tf_op jit(solution)/shard_map/reduce_scatter | solution.py:157
Sparse Core Ops, SparseCore 0:
  525.7 102.6 all-reduce.3
  632.3 76.6 reduce-scatter.9
  712.8 76.8 reduce-scatter.11
  793.0 72.5 reduce-scatter.7
where the time goes:
time: 897 us; the launch traced here: 894 us
  waiting for transfers between devices  302 us (34%)
  local copies, waits for them, and re-layouts  246 us (27%)
  other arithmetic  206 us (23%)
  matrix products  78.8 us (9%)
  starting transfers between devices  26.3 us (3%)
  blocking collectives  19.3 us (2%)
  between operations  15.6 us (2%)
    unnamed x7, waiting for transfers between devices  223 us
    scatter-add x1, other arithmetic, body(): grad_pool = jnp.zeros((pool_size, narrow), jnp.float32).at[trip_index.res...  186 us
    gather x1, local copies, waits for them, and re-layouts, body(): pool_red[trip_index]  115 us
    reduce_scatter x1, waiting for transfers between devices, body(): lax.psum_scatter((down_sum * factor).astype(jnp.bfloat16), 'graph', scatt...  75 us
    ppermute x8, starting transfers between devices, shifted(): return lax.ppermute(block, axis, route)  26.1 us
    convert_element_type x1, local copies, waits for them, and re-layouts, body(): outer = outer.astype(jnp.bfloat16).reshape(edges, basis_count * narrow)  25.6 us
    reshape x1, local copies, waits for them, and re-layouts, body(): grad_outer.reshape(edges, basis_count, narrow)  25.2 us
    unnamed x49, local copies, waits for them, and re-layouts  20.3 us
  transfers between devices with their start and end apart: 12, of which 6 were waited for; matrix products, arithmetic and copies ran while one was open for 7% of the time, Pallas kernels for 0%

commit v1 on v0

v1 whole, which is shorter than its diff:
```python
import functools
import math

import jax
import jax.numpy as jnp
from jax import lax
from jax.experimental import pallas as pl
from jax.experimental.pallas import tpu as pltpu
from jax.sharding import PartitionSpec as P

INV_ROOT = 0.7071067811865476
BF = jnp.bfloat16
F32 = jnp.float32
MESH = pl.DeviceIdType.MESH
VMEM_LIMIT = 56 * 1024 * 1024

E = 1024
K = 32
B = 112
TW = 64
D = 512
CAP = 256
NL = 4
G = 8
T = G * K


def offsets(count):
    return [(which // 2 + 1) * (1 - 2 * (which % 2)) for which in range(count)]


def shifted(block, axis, distance):
    n = lax.axis_size(axis)
    return lax.ppermute(block, axis, [((i - distance) % n, i) for i in range(n)])


def sigmoid(v):
    return 1.0 / (1.0 + jnp.exp(-v))


def silu(v):
    return v * sigmoid(v)


def slope(v):
    s = sigmoid(v)
    return s * (1.0 + v * (1.0 - s))


def iota(shape, dim):
    return lax.broadcasted_iota(jnp.int32, shape, dim)


def dot(a, b):
    return jnp.dot(a, b, preferred_element_type=F32)


def dot_nt(a, b):
    return lax.dot_general(a, b, (((1,), (1,)), ((), ())), preferred_element_type=F32)


def dot_tn(a, b):
    return lax.dot_general(a, b, (((0,), (0,)), ((), ())), preferred_element_type=F32)


def onehot(cond):
    return jnp.where(cond, 1.0, 0.0).astype(BF)


def front_kernel(msg, cot, w_edge, w_down, rows, count, *outs):
    pool_out = outs[0]
    red_out = outs[1:5]
    cot_out = outs[5:9]
    red = outs[9]

    for i in range(4):
        m = pl.ds(256 * i, 256)
        hidden = silu(dot(msg[m, :], w_edge[...])).astype(BF)
        red[m, :] = silu(dot(hidden, w_down[...])).astype(BF)
        r = red[m, :]
        pool_out[i] = jnp.concatenate([r[:128], r[128:]], axis=1)
    lane = iota((1, CAP), 1)
    lists = []
    for o in range(NL):
        lists.append(jnp.where(lane < count[0, o], rows[o : o + 1, :], -1))
    picks = jnp.concatenate(lists + lists, axis=0).T
    wide = iota((CAP, E), 1)
    for o in range(NL):
        hot = onehot(wide == picks[:, o : o + 1])
        r = dot(hot, red[...]).astype(BF)
        red_out[o][...] = jnp.concatenate([r[:128], r[128:]], axis=1)
        cot_out[o][...] = dot(hot, cot[...]).astype(BF)


def front(msg, cot, w_edge, w_down, rows, count):
    vm = pl.BlockSpec(memory_space=pltpu.VMEM)
    return pl.pallas_call(
        front_kernel,
        out_shape=[jax.ShapeDtypeStruct((4, 128, 128), BF)]
        + [jax.ShapeDtypeStruct((128, 128), BF)] * 4
        + [jax.ShapeDtypeStruct((CAP, D), BF)] * 4,
        in_specs=[vm] * 5 + [pl.BlockSpec(memory_space=pltpu.SMEM)],
        out_specs=[vm] * 9,
        scratch_shapes=[pltpu.VMEM((E, TW), BF)],
        compiler_params=pltpu.CompilerParams(vmem_limit_bytes=VMEM_LIMIT),
        name="front",
    )(msg, cot, w_edge, w_down, rows, count)


GS = 8
GP = 4
STEPS = E // (G * GS)


def load_w(wp, w_bil):
    wp[...] = jnp.zeros_like(wp)
    for ch in range(16):
        wp[128 * ch : 128 * ch + B, :] = w_bil[:, 256 * ch : 256 * ch + 256]


def fwd_kernel(basis, idx, pool, r0, r1, r2, r3, w_bil, outer, bas, state, pool_t, wp, sbuf):
    @pl.when(pl.program_id(0) == 0)
    def _():
        load_w(wp, w_bil)
        for hi in range(8):
            src = pool[hi] if hi < 4 else (r0, r1, r2, r3)[hi - 4][...]
            flip = src.astype(F32).T
            pool_t[64 * hi : 64 * hi + 64, :] = jnp.concatenate(
                [flip[:64], flip[64:]], axis=1
            ).astype(BF)

    e_lane = lax.rem(iota((16, T), 1), G)
    quad = iota((16, T), 0) // 4
    keep = [onehot(e_lane == 4 * q + quad) for q in range(2)]
    low = iota((8, T), 0) < 4

    def some(j, carry):
        hots, his = [], []
        for i in range(GP):
            row = idx[pl.ds(j * GP + i, 1), :]
            hots.append(onehot(iota((256, T), 0) == jnp.bitwise_and(row, 255)))
            his.append(jnp.right_shift(row, 8))
        found = dot(pool_t[...], jnp.concatenate(hots, axis=1))
        for i in range(GP):
            g = j * GP + i
            wide = basis[pl.ds(pl.multiple_of(g * G, G), G), :].astype(F32)
            pieces = []
            for k in range(K):
                piece = wide[:, k * B : (k + 1) * B]
                pieces.append(jnp.concatenate([piece, jnp.zeros((G, 128 - B), F32)], axis=1))
            rhs = jnp.concatenate(pieces, axis=0).astype(BF)
            bas[pl.ds(pl.multiple_of(g * T, T), T), :] = rhs
            got = jnp.zeros((TW, T), F32)
            for hi in range(8):
                part = found[64 * hi : 64 * hi + 64, T * i : T * i + T]
                got = jnp.where(his[i] == hi, part, got)
            tiles = []
            for v in range(8):
                x = got[8 * v : 8 * v + 8]
                y = pltpu.roll(x, 4, 0)
                for d in (jnp.where(low, x, y), jnp.where(low, y, x)):
                    tiles.append(jnp.concatenate([d, d], axis=0).astype(BF))
            lhs = jnp.concatenate([t * keep[q] for q in range(2) for t in tiles], axis=0)
            out = dot(lhs, rhs).astype(BF)
            for q in range(2):
                for ch in range(16):
                    at = (q * 16 + ch) * 16
                    outer[pl.ds(pl.multiple_of(g * 32 + 16 * q, 16), 16), 128 * ch : 128 * ch + 128] = (
                        out[at : at + 16]
                    )
        return carry

    lax.fori_loop(0, GS // GP, some, 0)
    rows = 32 * GS
    full = dot(outer[...], wp[...])
    full = jnp.where(lax.rem(iota((rows, 256), 0), 4) == iota((rows, 256), 1) // 64, full, 0.0)
    full = full + pltpu.roll(full, 1, 0)
    full = full + pltpu.roll(full, 2, 0)
    sbuf[...] = full[:, :128] + full[:, 128:]
    picked = sbuf[pl.ds(3, G * GS, stride=4), :]
    state[...] = (picked + pltpu.roll(picked, 64, 1)).astype(BF)


def fwd(basis, idx, pool, recv, w_bil):
    whole = lambda shape: pl.BlockSpec(shape, lambda i: (0,) * len(shape))
    return pl.pallas_call(
        fwd_kernel,
        grid=(STEPS,),
        out_shape=[
            jax.ShapeDtypeStruct((4 * E, 2048), BF),
            jax.ShapeDtypeStruct((E * K, 128), BF),
            jax.ShapeDtypeStruct((E, 128), BF),
        ],
        in_specs=[
            pl.BlockSpec((G * GS, K * B), lambda i: (i, 0)),
            pl.BlockSpec((GS, T), lambda i: (i, 0)),
            whole((4, 128, 128)),
        ]
        + [whole((128, 128))] * 4
        + [whole((B, 4096))],
        out_specs=[
            pl.BlockSpec((32 * GS, 2048), lambda i: (i, 0)),
            pl.BlockSpec((T * GS, 128), lambda i: (i, 0)),
            pl.BlockSpec((G * GS, 128), lambda i: (i, 0)),
        ],
        scratch_shapes=[
            pltpu.VMEM((512, 256), BF),
            pltpu.VMEM((2048, 256), BF),
            pltpu.VMEM((32 * GS, 128), F32),
        ],
        compiler_params=pltpu.CompilerParams(vmem_limit_bytes=VMEM_LIMIT),
        cost_estimate=pl.CostEstimate(flops=2 * 10**10, bytes_accessed=3 * 10**7, transcendentals=0),
        name="triplets_out",
    )(basis, idx, pool, *recv, w_bil)


BE = 128


def mid_kernel(factor, state, outer, cot, all_cot, c0, c1, c2, c3, rev, w_up, count, gsx, early, bil, up):
    step = pl.program_id(0)

    @pl.when(step == 0)
    def _():
        bil[...] = jnp.zeros_like(bil)
        up[...] = jnp.zeros_like(up)

    st = state[...][:, :TW]
    alive = iota((BE, D), 0) + step * BE < count[0, 0]
    scaled = jnp.where(alive, cot[...].astype(F32) * INV_ROOT, 0.0)
    grad_ca = (scaled * slope(dot(st, w_up[0]))).astype(BF)
    row = rev[pl.ds(step, 1), :]
    col = jnp.concatenate([row] * 8, axis=0).T[:, :1]
    mirror = dot(onehot(iota((BE, E), 1) == col), all_cot[...])
    for o, c in enumerate((c0, c1, c2, c3)):
        mirror = mirror + dot(onehot(iota((BE, CAP), 1) + (E + CAP * o) == col), c[...])
    grad_ac = (mirror * INV_ROOT * slope(dot(st, w_up[1]))).astype(BF)
    up[:TW, :] += dot_tn(st, grad_ca)
    up[TW:, :] += dot_tn(st, grad_ac)
    own = dot_nt(grad_ca, jnp.concatenate([w_up[0]] * 4, axis=0))
    back = dot_nt(grad_ac, jnp.concatenate([w_up[1]] * 4, axis=0)).astype(BF)
    grad_state = (own + back.astype(F32)).astype(BF)
    spread = onehot(iota((4 * BE, BE), 0) // 4 == iota((4 * BE, BE), 1))
    big = dot(spread, grad_state)
    big = jnp.where(lax.rem(iota((4 * BE, 256), 0), 4) == iota((4 * BE, 256), 1) // 64, big, 0.0)
    big = big.astype(BF)
    gsx[...] = big
    bil[...] += dot_tn(big, outer[...])

    @pl.when(step == pl.num_programs(0) - 1)
    def _():
        turned = (up[...] * factor).T.astype(BF)
        for i in range(32):
            early[i, :, 1024:1152] = turned[16 * i : 16 * i + 16]
            r, c = (i % 2) * 128, (i // 2) * 128
            for j in range(8):
                early[i, :, 128 * j : 128 * j + 128] = (
                    bil[r + 16 * j : r + 16 * j + 16, c : c + 128] * factor
                ).astype(BF)


def mid(factor, state, outer, cot, recv, rev, w_up, count):
    whole = lambda shape: pl.BlockSpec(shape, lambda i: (0,) * len(shape))
    return pl.pallas_call(
        functools.partial(mid_kernel, factor),
        grid=(E // BE,),
        out_shape=[
            jax.ShapeDtypeStruct((4 * E, 256), BF),
            jax.ShapeDtypeStruct((32, 16, 1152), BF),
        ],
        in_specs=[
            pl.BlockSpec((BE, 128), lambda i: (i, 0)),
            pl.BlockSpec((4 * BE, 2048), lambda i: (i, 0)),
            pl.BlockSpec((BE, D), lambda i: (i, 0)),
            whole((E, D)),
        ]
        + [whole((CAP, D))] * 4
        + [whole((8, 128)), whole((2, TW, D)), pl.BlockSpec(memory_space=pltpu.SMEM)],
        out_specs=[
            pl.BlockSpec((4 * BE, 256), lambda i: (i, 0)),
            whole((32, 16, 1152)),
        ],
        scratch_shapes=[pltpu.VMEM((256, 2048), F32), pltpu.VMEM((2 * TW, D), F32)],
        compiler_params=pltpu.CompilerParams(vmem_limit_bytes=VMEM_LIMIT),
        name="middle",
    )(state, outer, cot, cot, *recv, rev, w_up, count)


def bwd_kernel(gsx, bas, idx, w_bil, local, b0, b1, b2, b3, wp, go, acc):
    step = pl.program_id(0)

    @pl.when(step == 0)
    def _():
        load_w(wp, w_bil)
        acc[...] = jnp.zeros_like(acc)

    go[...] = dot_nt(gsx[...], wp[...]).astype(BF)
    e_lane = lax.rem(iota((8, T), 1), G)
    pair = e_lane // 2
    odd = lax.rem(e_lane, 2) == 1
    stay = (iota((8, T), 0) >= 4) == odd

    def some(j, carry):
        hots, sides = [], []
        for i in range(GP):
            g = j * GP + i
            row = idx[pl.ds(g, 1), :]
            hots.append(onehot(iota((256, T), 0) == jnp.bitwise_and(row, 255)))
            hi_of = jnp.right_shift(row, 8)
            lhs = jnp.concatenate(
                [
                    go[pl.ds(pl.multiple_of(g * 32 + 16 * q, 16), 16), 128 * ch : 128 * ch + 128]
                    for q in range(2)
                    for ch in range(16)
                ],
                axis=0,
            )
            full = dot_nt(lhs, bas[pl.ds(pl.multiple_of(g * T, T), T), :])
            picked = []
            for ch in range(16):
                z = full[16 * ch : 16 * ch + 8]
                for p in range(1, 4):
                    at = (p // 2) * 256 + 16 * ch + 8 * (p % 2)
                    z = jnp.where(pair == p, full[at : at + 8], z)
                picked.append(z)
            grads = []
            for v in range(8):
                z0, z1 = picked[2 * v], picked[2 * v + 1]
                here = jnp.where(odd, z1, z0)
                there = jnp.where(odd, z0, z1)
                grads.append(jnp.where(stay, here, pltpu.roll(there, 4, 0)))
            grad = jnp.concatenate(grads, axis=0).astype(BF)
            sides.append(
                jnp.concatenate([grad * onehot(hi_of == hi) for hi in range(8)], axis=0)
            )
        acc[...] += dot_nt(jnp.concatenate(sides, axis=1), jnp.concatenate(hots, axis=1))
        return carry

    lax.fori_loop(0, GS // GP, some, 0)

    @pl.when(step == pl.num_programs(0) - 1)
    def _():
        for hi in range(8):
            part = acc[64 * hi : 64 * hi + 64, :]
            flip = jnp.concatenate([part[:, :128], part[:, 128:]], axis=0).T
            if hi < 4:
                local[hi] = flip
            else:
                (b0, b1, b2, b3)[hi - 4][...] = flip.astype(BF)


def bwd(gsx, bas, idx, w_bil):
    whole = lambda shape: pl.BlockSpec(shape, lambda i: (0,) * len(shape))
    return pl.pallas_call(
        bwd_kernel,
        grid=(STEPS,),
        out_shape=[jax.ShapeDtypeStruct((4, 128, 128), F32)]
        + [jax.ShapeDtypeStruct((128, 128), BF)] * 4,
        in_specs=[
            pl.BlockSpec((32 * GS, 256), lambda i: (i, 0)),
            pl.BlockSpec((T * GS, 128), lambda i: (i, 0)),
            pl.BlockSpec((GS, T), lambda i: (i, 0)),
            whole((B, 4096)),
        ],
        out_specs=[whole((4, 128, 128))] + [whole((128, 128))] * 4,
        scratch_shapes=[
            pltpu.VMEM((2048, 256), BF),
            pltpu.VMEM((32 * GS, 2048), BF),
            pltpu.VMEM((512, 256), F32),
        ],
        compiler_params=pltpu.CompilerParams(vmem_limit_bytes=VMEM_LIMIT),
        name="triplets_back",
    )(gsx, bas, idx, w_bil)


def tail_kernel(factor, msg, w_edge, w_down, rows, count, local, b0, b1, b2, b3, grad_msg, late, gred, edge, down):
    lane = iota((1, CAP), 1)
    hots, backs = [], []
    for o, b in enumerate((b0, b1, b2, b3)):
        picks = jnp.where(lane < count[0, o], rows[o : o + 1, :], -1)
        hots.append(onehot(iota((E, CAP), 0) == picks))
        back = b[...]
        backs.append(jnp.concatenate([back[:, :TW], back[:, TW:]], axis=0))
    gred[...] = dot(jnp.concatenate(hots, axis=1), jnp.concatenate(backs, axis=0))
    for i in range(4):
        m = pl.ds(256 * i, 256)
        own = local[i]
        total = gred[m, :] + jnp.concatenate([own[:, :TW], own[:, TW:]], axis=0)
        pre_edge = dot(msg[m, :], w_edge[...])
        hidden = silu(pre_edge).astype(BF)
        pre_down = dot(hidden, w_down[...])
        grad_down = (total * slope(pre_down)).astype(BF)
        grad_hidden = dot_nt(grad_down, w_down[...])
        grad_edge = (grad_hidden * slope(pre_edge)).astype(BF)
        grad_msg[m, :] = dot_nt(grad_edge, w_edge[...]).astype(BF)
        d = dot_tn(hidden, grad_down)
        e = dot_tn(msg[m, :], grad_edge)
        if i == 0:
            edge[...] = e
            down[...] = d
        else:
            edge[...] += e
            down[...] += d
    both = jnp.concatenate(
        [edge[...] * factor, down[...] * factor, jnp.zeros((D, TW), F32)], axis=1
    ).astype(BF)
    for i in range(32):
        late[i] = both[16 * i : 16 * i + 16]


def tail(factor, msg, w_edge, w_down, rows, count, local, back):
    vm = pl.BlockSpec(memory_space=pltpu.VMEM)
    return pl.pallas_call(
        functools.partial(tail_kernel, factor),
        out_shape=[
            jax.ShapeDtypeStruct((E, D), BF),
            jax.ShapeDtypeStruct((32, 16, 640), BF),
        ],
        in_specs=[vm] * 4 + [pl.BlockSpec(memory_space=pltpu.SMEM)] + [vm] * 5,
        out_specs=[vm] * 2,
        scratch_shapes=[
            pltpu.VMEM((E, TW), F32),
            pltpu.VMEM((D, D), F32),
            pltpu.VMEM((D, TW), F32),
        ],
        compiler_params=pltpu.CompilerParams(vmem_limit_bytes=VMEM_LIMIT),
        name="tail",
    )(msg, w_edge, w_down, rows, count, local, *back)


def sum_kernel(n, n_dp, early, late, o_edge, o_down, o_bil, o_up,
               in_e, in_l, mine_e, mine_l, dp_e, dp_l, send, recv, dp_send, dp_recv):
    me = lax.axis_index("graph")
    dp = lax.axis_index("dp")

    barrier = pltpu.get_barrier_semaphore()

    def greet(d, carry):
        pl.semaphore_signal(
            barrier, inc=1, device_id=(dp, lax.rem(me + d, n)), device_id_type=MESH
        )
        return carry

    lax.fori_loop(1, n, greet, 0)
    for d in range(1, n_dp):
        pl.semaphore_signal(
            barrier, inc=1, device_id=(lax.rem(dp + d, n_dp), me), device_id_type=MESH
        )
    pl.semaphore_wait(barrier, n - 1 + n_dp - 1)

    def pair(d):
        to = lax.rem(me + d, n)
        where = (dp, to)
        return (
            pltpu.make_async_remote_copy(
                early.at[to], in_e.at[d], send.at[0, d], recv.at[0, d],
                device_id=where, device_id_type=MESH),
            pltpu.make_async_remote_copy(
                late.at[to], in_l.at[d], send.at[1, d], recv.at[1, d],
                device_id=where, device_id_type=MESH),
        )

    def go(d, carry):
        for c in pair(d):
            c.start()
        return carry

    lax.fori_loop(1, n, go, 0)
    mine_e[...] = early[me].astype(F32)
    mine_l[...] = late[me].astype(F32)

    def take(d, carry):
        for c in pair(d):
            c.wait_recv()
        mine_e[...] += in_e[d].astype(F32)
        mine_l[...] += in_l[d].astype(F32)
        return carry

    lax.fori_loop(1, n, take, 0)
    dp_e[0] = mine_e[...].astype(BF)
    dp_l[0] = mine_l[...].astype(BF)
    swaps = []
    for d in range(1, n_dp):
        where = (lax.rem(dp + d, n_dp), me)
        swaps.append(pltpu.make_async_remote_copy(
            dp_e.at[0], dp_e.at[d], dp_send.at[0, d], dp_recv.at[0, d],
            device_id=where, device_id_type=MESH))
        swaps.append(pltpu.make_async_remote_copy(
            dp_l.at[0], dp_l.at[d], dp_send.at[1, d], dp_recv.at[1, d],
            device_id=where, device_id_type=MESH))
    for c in swaps:
        c.start()

    def done(d, carry):
        for c in pair(d):
            c.wait_send()
        return carry

    lax.fori_loop(1, n, done, 0)
    for c in swaps:
        c.wait()
    def total(buf):
        terms = []
        for d in range(n_dp):
            terms.append(buf[d].astype(F32))
        out = jnp.zeros_like(terms[0])
        for source in range(n_dp):
            for d in range(n_dp):
                hit = lax.rem(dp + n_dp - d, n_dp) == source
                out = out + jnp.where(hit, terms[d], 0.0)
        return out

    e = total(dp_e)
    l = total(dp_l)
    o_edge[...] = l[:, :D]
    o_down[...] = l[:, D : D + TW]
    square = jnp.concatenate([e[:, 128 * j : 128 * j + 128] for j in range(8)], axis=0).T
    o_bil[...] = square[:B]
    o_up[...] = e[:, 1024:1152].T


def summed(early, late):
    n = lax.axis_size("graph")
    n_dp = lax.axis_size("dp")
    vm = pl.BlockSpec(memory_space=pltpu.VMEM)
    return pl.pallas_call(
        functools.partial(sum_kernel, n, n_dp),
        out_shape=[
            jax.ShapeDtypeStruct((16, D), F32),
            jax.ShapeDtypeStruct((16, TW), F32),
            jax.ShapeDtypeStruct((B, 128), F32),
            jax.ShapeDtypeStruct((128, 16), F32),
        ],
        in_specs=[vm] * 2,
        out_specs=[vm] * 4,
        scratch_shapes=[
            pltpu.VMEM((n, 16, 1152), BF),
            pltpu.VMEM((n, 16, 640), BF),
            pltpu.VMEM((16, 1152), F32),
            pltpu.VMEM((16, 640), F32),
            pltpu.VMEM((n_dp, 16, 1152), BF),
            pltpu.VMEM((n_dp, 16, 640), BF),
            pltpu.SemaphoreType.DMA((2, n)),
            pltpu.SemaphoreType.DMA((2, n)),
            pltpu.SemaphoreType.DMA((2, n_dp)),
            pltpu.SemaphoreType.DMA((2, n_dp)),
        ],
        compiler_params=pltpu.CompilerParams(
            collective_id=0, has_side_effects=True, vmem_limit_bytes=VMEM_LIMIT
        ),
        name="weight_sums",
    )(early, late)


def body(
    messages, cotangent, triplet_basis, w_edge, w_down, w_bil, w_up,
    trip_src, send_rows, send_count, rev_src, edge_count,
):
    msg, cot = messages[0], cotangent[0]
    factor = 1.0 / math.sqrt(lax.axis_size("dp") * lax.axis_size("graph") * E)
    shifts = offsets(NL)
    idx = trip_src[0].reshape(E // G, G, K).transpose(0, 2, 1).reshape(E // G, T)
    outs = front(msg, cot, w_edge, w_down, send_rows[0], send_count)
    pool, red_send, cot_send = outs[0], outs[1:5], outs[5:9]
    red_recv = [shifted(red_send[o], "graph", shifts[o]) for o in range(NL)]
    cot_recv = [shifted(cot_send[o], "graph", shifts[o]) for o in range(NL)]
    outer, bas, state = fwd(triplet_basis[0], idx, pool, red_recv, w_bil)
    gsx, early = mid(
        factor, state, outer, cot, cot_recv, rev_src.reshape(8, 128), w_up, edge_count
    )
    outs = bwd(gsx, bas, idx, w_bil)
    back = [shifted(outs[1 + o], "graph", -shifts[o]) for o in range(NL)]
    grad_msg, late = tail(
        factor, msg, w_edge, w_down, send_rows[0], send_count, outs[0], back
    )
    g_edge, g_down, g_bil, g_up = summed(early, late)
    return grad_msg[None], g_edge, g_down, g_bil, g_up.reshape(2, TW, 16)


def solution(mesh):
    row = P("dp", "graph", None)
    flat = P("dp", "graph")
    return jax.shard_map(
        body,
        mesh=mesh,
        in_specs=(row, row, row, P(), P(), P(), P(), row, row, flat, flat, flat),
        out_specs=(
            row,
            P("graph", None),
            P("graph", None),
            P(None, "graph"),
            P(None, None, "graph"),
        ),
        check_vma=False,
    )
```

time: 897 us -> 197 us (0.22)
  waiting for transfers between devices: 302 us -> 5.47 us
  local copies, waits for them, and re-layouts: 246 us -> 11.4 us
  other arithmetic: 206 us -> 0 us
  Pallas kernels: 0 us -> 153 us
  matrix products: 78.8 us -> 0 us
  blocking collectives: 19.3 us -> 0 us
  between operations: 15.6 us -> 1.43 us
    unnamed x7 -> x0, waiting for transfers between devices: 223 us -> none
    scatter-add x2 -> x0, other arithmetic: 194 us -> none  [the longest x1 186 us: body(): grad_pool = jnp.zeros((pool_size, narrow), jnp.float32).at[trip_index.res...]
    pallas_call x0 -> x6, Pallas kernels: none -> 153 us  [the longest x1 43.4 us: summed(): pl.pallas_call(functools.partial(sum_kernel, n, n_dp), out_shape=[jax.Sha...]
    gather x5 -> x0, local copies, waits for them, and re-layouts: 129 us -> none  [the longest x1 115 us: body(): pool_red[trip_index]]
    dot_general x17 -> x0, matrix products: 78.8 us -> none  [the longest x1 20.1 us: body(): jnp.einsum('ebc,ekb->ekc', grad_outer.reshape(edges, basis_count, narrow)...]
    reduce_scatter x1 -> x0, waiting for transfers between devices: 75 us -> none  [body(): lax.psum_scatter((down_sum * factor).astype(jnp.bfloat16), 'graph', scatt...]
    convert_element_type x6 -> x0, local copies, waits for them, and re-layouts: 50.8 us -> none  [the longest x1 25.6 us: body(): outer = outer.astype(jnp.bfloat16).reshape(edges, basis_count * narrow)]
    reshape x2 -> x1, local copies, waits for them, and re-layouts: 29 us -> 0.76 us  [body(): trip_src[0].reshape(E // G, G, K).transpose(0, 2, 1).reshape(E // G, T)]
  transfers between devices with their start and end apart: 12 -> 12, of which waited for: 6 -> 2; matrix products, arithmetic and copies ran while one was open for 7% -> 1% of each run, Pallas kernels for 0% -> 18%
where the time goes in v1:
time: 197 us; the launch traced here: 196 us
  Pallas kernels  153 us (78%)
  starting transfers between devices  24.1 us (12%)
  local copies, waits for them, and re-layouts  11.4 us (6%)
  waiting for transfers between devices  5.47 us (3%)
    pallas_call x1, Pallas kernels, summed(): pl.pallas_call(functools.partial(sum_kernel, n, n_dp), out_shape=[jax.Sha...  43.4 us
    pallas_call x1, Pallas kernels, bwd(): pl.pallas_call(bwd_kernel, grid=(STEPS,), out_shape=[jax.ShapeDtypeStruct...  40.8 us
    pallas_call x1, Pallas kernels, fwd(): pl.pallas_call(fwd_kernel, grid=(STEPS,), out_shape=[jax.ShapeDtypeStruct...  35.3 us
    ppermute x12, starting transfers between devices, shifted(): lax.ppermute(block, axis, [((i - distance) % n, i) for i in range(n)])  24.1 us
    pallas_call x1, Pallas kernels, mid(): pl.pallas_call(functools.partial(mid_kernel, factor), grid=(E // BE,), ou...  20.8 us
    unnamed x30, local copies, waits for them, and re-layouts  10.4 us
    pallas_call x1, Pallas kernels, tail(): pl.pallas_call(functools.partial(tail_kernel, factor), out_shape=[jax.Sha...  7.05 us
    pallas_call x1, Pallas kernels, front(): pl.pallas_call(front_kernel, out_shape=[jax.ShapeDtypeStruct((4, 128, 128...  5.85 us
  transfers between devices with their start and end apart: 12, of which 2 were waited for; matrix products, arithmetic and copies ran while one was open for 1% of the time, Pallas kernels for 18%

profile of v1, /device:TPU:0, one launch (start us, length us, event | category | flops | bytes accessed | tf_op | source)
XLA Modules:
  0.0 195.5 jit_solution(7116466404569503076)
XLA Ops:
  0.6 1.6 copy.26.w_down
  2.2 5.9 %front.1 = (bf16[4,128,128]{2,1,0:T(8,128)(2,1)}, bf16[128,128]{1,0:T(8,128)(2,1)}, bf16[128,128]{1,0:T(8,128)(2,1)}, bf16[128,128]{1,0:T(8,128)(2,1)}, bf16[128...) custom-call(bf16[1024,512]{1,0:T(8,128)(2,1)} %bitcast.14, ...), custom_call_target="tpu_custom_call" | custom-call | tf_op jit(solution)/shard_map/front/pallas_call | solution.py:97
  8.1 0.0 collective-permute-start
  8.1 5.8 %collective-permute-start.1 = (bf16[128,128]{1,0:T(8,128)(2,1)}, bf16[128,128]{1,0:T(8,128)(2,1)S(1)}, u32[]{:S(2)}, u32[]{:S(2)}) collective-permute-start(bf16[128,128]{1,0:T(8,128)(2,1)} %get-tuple-element.32), channel_id=1, source_target_pairs={{1,0},{2,1},{3,2},{4,3},{5,4},{6,5},{7,6},{8,7},{9,8},{10,9},{11,1... | collective-permute-start | bytes 98312 | tf_op jit(solution)/shard_map/ppermute | solution.py:34
  13.8 0.0 collective-permute-start.2
  13.8 5.3 %collective-permute-start.3 = (bf16[128,128]{1,0:T(8,128)(2,1)}, bf16[128,128]{1,0:T(8,128)(2,1)S(1)}, u32[]{:S(2)}, u32[]{:S(2)}) collective-permute-start(bf16[128,128]{1,0:T(8,128)(2,1)} %get-tuple-element.34), channel_id=1, source_target_pairs={{2,0},{3,1},{4,2},{5,3},{6,4},{7,5},{8,6},{9,7},{10,8},{11,9},{12,... | collective-permute-start | bytes 98312 | tf_op jit(solution)/shard_map/ppermute | solution.py:34
  19.2 0.0 collective-permute-start.4
  19.8 1.1 copy.21
  20.9 0.2 copy.22
  21.2 0.8 copy.24.idx
  21.9 0.0 collective-permute-done.r0
  21.9 0.0 copy-start.8
  21.9 5.1 %collective-permute-start.5 = (bf16[256,512]{1,0:T(8,128)(2,1)}, bf16[256,512]{1,0:T(8,128)(2,1)S(1)}, u32[]{:S(2)}, u32[]{:S(2)}) collective-permute-start(bf16[256,512]{1,0:T(8,128)(2,1)} %get-tuple-element.38), channel_id=1, source_target_pairs={{1,0},{2,1},{3,2},{4,3},{5,4},{6,5},{7,6},{8,7},{9,8},{10,9},{11,1... | collective-permute-start | bytes 786440 | tf_op jit(solution)/shard_map/ppermute | solution.py:34
  27.0 0.0 collective-permute-done.1.r1
  27.0 0.0 copy-start.9
  27.0 0.0 collective-permute-start.6
  27.0 0.0 collective-permute-done.2.r2
  27.0 0.0 copy-start.10
  27.0 5.3 %collective-permute-start.7 = (bf16[256,512]{1,0:T(8,128)(2,1)}, bf16[256,512]{1,0:T(8,128)(2,1)S(1)}, u32[]{:S(2)}, u32[]{:S(2)}) collective-permute-start(bf16[256,512]{1,0:T(8,128)(2,1)} %get-tuple-element.40), channel_id=1, source_target_pairs={{2,0},{3,1},{4,2},{5,3},{6,4},{7,5},{8,6},{9,7},{10,8},{11,9},{12,... | collective-permute-start | bytes 786440 | tf_op jit(solution)/shard_map/ppermute | solution.py:34
  32.4 0.0 collective-permute-done.3.r3
  32.4 0.0 copy-start.11
  32.4 0.0 copy-done.8
  32.4 0.0 copy-done.9
  32.4 0.0 copy-done.10
  32.4 0.6 copy-done.11
  33.0 35.3 %triplets_out.1 = (bf16[4096,2048]{1,0:T(8,128)(2,1)}, bf16[32768,128]{1,0:T(8,128)(2,1)}, bf16[1024,128]{1,0:T(8,128)(2,1)}) custom-call(bf16[1024,3584]{1,0:T(8,128)(2,1)} %bitcast.22, s32[128,256]{1,0:T(8,128)} %copy.24.idx, bf16[4,128,128]{2,1,0:T(8,128)(2,1)} %get-tuple-element.30.pool, bf16[128,128]{1,0:T(8,128)(2,1)} %copy-done.8, ...), custom_call_target="tpu_custom_call" | custom-call | flops 20000000000 | bytes 30000000 | tf_op jit(solution)/shard_map/triplets_out/pallas_call | solution.py:186
  68.2 0.0 collective-permute-done.4.c0
  68.2 0.0 copy-start
  68.2 0.0 collective-permute-done.5.c1
  68.3 0.0 copy-start.1
  68.3 0.0 collective-permute-done.6.c2
  68.3 0.0 copy-start.2
  68.3 0.0 collective-permute-done.7.c3
  68.3 0.0 copy-start.3
  68.3 0.6 copy-done
  68.9 0.1 copy-done.1
  69.0 0.1 copy-done.2
  69.1 0.1 copy-done.3
  69.2 20.8 %middle.1 = (bf16[4096,256]{1,0:T(8,128)(2,1)}, bf16[32,16,1152]{2,1,0:T(8,128)(2,1)}) custom-call(bf16[1024,128]{1,0:T(8,128)(2,1)} %get-tuple-element.35.state, bf16[4096,2048]{1,0:T(8,128)(2,1)} %get-tuple-element.36.outer, bf16[1024,512]{1,0:T(8,128)(2,1)} %bitcast.12, bf16[1024,512]{1,0:T(8,128)(2,1)} %bitcast.13, bf16[256,512]{1,0:T(8,128)(2,1)} %copy-done, ...), custom_call_target="tpu_custom_call" | custom-call | tf_op jit(solution)/shard_map/middle/pallas_call | solution.py:264
  90.0 40.8 %triplets_back.1 = (f32[4,128,128]{2,1,0:T(8,128)}, bf16[128,128]{1,0:T(8,128)(2,1)}, bf16[128,128]{1,0:T(8,128)(2,1)}, bf16[128,128]{1,0:T(8,128)(2,1)}, bf16[128,128]{1,0:T(8,128)(2,1)}) custom-call(bf16[4096,256]{1,0:T(8,128)(2,1)} %get-tuple-element.41.gsx, bf16[32768,128]{1,0:T(8,128)(2,1)} %get-tuple-element.42.bas, s32[128,256]{1,0:T(8,128)} %copy.24.idx, ...), custom_call_target="tpu_custom_call" | custom-call | tf_op jit(solution)/shard_map/triplets_back/pallas_call | solution.py:354
  130.8 0.1 collective-permute-start.8
  130.9 0.5 collective-permute-start.9
  131.4 0.0 collective-permute-start.10
  131.4 2.0 %collective-permute-start.11 = (bf16[128,128]{1,0:T(8,128)(2,1)}, bf16[128,128]{1,0:T(8,128)(2,1)S(1)}, u32[]{:S(2)}, u32[]{:S(2)}) collective-permute-start(bf16[128,128]{1,0:T(8,128)(2,1)} %get-tuple-element.47), channel_id=1, source_target_pairs={{30,0},{31,1},{0,2},{1,3},{2,4},{3,5},{4,6},{5,7},{6,8},{7,9},{8,1... | collective-permute-start | bytes 98312 | tf_op jit(solution)/shard_map/ppermute | solution.py:34
  133.4 0.0 collective-permute-done.8.b0
  133.4 0.0 copy-start.4
  133.4 4.4 %collective-permute-done.9.b1 = bf16[128,128]{1,0:T(8,128)(2,1)S(1)} collective-permute-done((bf16[128,128]{1,0:T(8,128)(2,1)}, bf16[128,128]{1,0:T(8,128)(2,1)S(1)}, u32[]{:S(2)}, u32[]{:S(2)}) %collective-permute-start.9) | collective-permute-done | bytes 32800 | tf_op jit(solution)/shard_map/ppermute | solution.py:34
  137.8 0.0 copy-start.5
  137.8 0.0 collective-permute-done.10.b2
  137.8 0.0 copy-start.6
  137.8 1.0 collective-permute-done.11.b3
  138.9 0.0 copy-start.7
  138.9 0.0 copy-done.4
  138.9 0.0 copy-done.5
  138.9 0.0 copy-done.6
  138.9 0.6 copy-done.7
  139.5 7.1 %tail.1 = (bf16[1024,512]{1,0:T(8,128)(2,1)}, bf16[32,16,640]{2,1,0:T(8,128)(2,1)}) custom-call(bf16[1024,512]{1,0:T(8,128)(2,1)} %bitcast.15, bf16[512,512]{1,0:T(8,128)(2,1)} %w_edge.3, bf16[512,64]{1,0:T(8,128)(2,1)} %copy.26.w_down, s32[4,256]{1,0:T(4,128)} %bitcast.20, s32[1,4]{1,0:T(1,128)} %count.4, f32[4,128,128]{2,1,0:T(8,128)} %get-tuple-element.43.local, ...), custom_call_target="tpu_custom_call" | custom-call | tf_op jit(solution)/shard_map/tail/pallas_call | solution.py:413
  146.5 43.4 %weight_sums.1 = (f32[16,512]{1,0:T(8,128)}, f32[16,64]{1,0:T(8,128)}, f32[112,128]{1,0:T(8,128)}, f32[128,16]{1,0:T(8,128)}) custom-call(bf16[32,16,1152]{2,1,0:T(8,128)(2,1)} %get-tuple-element.49.early, bf16[32,16,640]{2,1,0:T(8,128)(2,1)} %get-tuple-element.50.late), custom_call_target="tpu_custom_call" | custom-call | tf_op jit(solution)/shard_map/weight_sums/pallas_call | solution.py:526
  189.9 1.5 copy.27
  191.4 1.4 copy.32
  192.8 1.3 copy.33
  194.1 1.4 copy.34
Async XLA Ops:
  8.1 13.9 %collective-permute-start = (bf16[128,128]{1,0:T(8,128)(2,1)}, bf16[128,128]{1,0:T(8,128)(2,1)S(1)}, u32[]{:S(2)}, u32[]{:S(2)}) collective-permute-start(bf16[128,128]{1,0:T(8,128)(2,1)} %get-tuple-element.31), channel_id=1, source_target_pairs={{31,0},{0,1},{1,2},{2,3},{3,4},{4,5},{5,6},{6,7},{7,8},{8,9},{9,10... | collective-permute-start | bytes 98312 | tf_op jit(solution)/shard_map/ppermute | solution.py:34
  8.1 18.9 %collective-permute-start.1 = (bf16[128,128]{1,0:T(8,128)(2,1)}, bf16[128,128]{1,0:T(8,128)(2,1)S(1)}, u32[]{:S(2)}, u32[]{:S(2)}) collective-permute-start(bf16[128,128]{1,0:T(8,128)(2,1)} %get-tuple-element.32), channel_id=1, source_target_pairs={{1,0},{2,1},{3,2},{4,3},{5,4},{6,5},{7,6},{8,7},{9,8},{10,9},{11,1... | collective-permute-start | bytes 98312 | tf_op jit(solution)/shard_map/ppermute | solution.py:34
  13.8 13.2 %collective-permute-start.2 = (bf16[128,128]{1,0:T(8,128)(2,1)}, bf16[128,128]{1,0:T(8,128)(2,1)S(1)}, u32[]{:S(2)}, u32[]{:S(2)}) collective-permute-start(bf16[128,128]{1,0:T(8,128)(2,1)} %get-tuple-element.33), channel_id=1, source_target_pairs={{30,0},{31,1},{0,2},{1,3},{2,4},{3,5},{4,6},{5,7},{6,8},{7,9},{8,1... | collective-permute-start | bytes 98312 | tf_op jit(solution)/shard_map/ppermute | solution.py:34
  13.8 18.5 %collective-permute-start.3 = (bf16[128,128]{1,0:T(8,128)(2,1)}, bf16[128,128]{1,0:T(8,128)(2,1)S(1)}, u32[]{:S(2)}, u32[]{:S(2)}) collective-permute-start(bf16[128,128]{1,0:T(8,128)(2,1)} %get-tuple-element.34), channel_id=1, source_target_pairs={{2,0},{3,1},{4,2},{5,3},{6,4},{7,5},{8,6},{9,7},{10,8},{11,9},{12,... | collective-permute-start | bytes 98312 | tf_op jit(solution)/shard_map/ppermute | solution.py:34
  19.2 49.0 %collective-permute-start.4 = (bf16[256,512]{1,0:T(8,128)(2,1)}, bf16[256,512]{1,0:T(8,128)(2,1)S(1)}, u32[]{:S(2)}, u32[]{:S(2)}) collective-permute-start(bf16[256,512]{1,0:T(8,128)(2,1)} %get-tuple-element.37), channel_id=1, source_target_pairs={{31,0},{0,1},{1,2},{2,3},{3,4},{4,5},{5,6},{6,7},{7,8},{8,9},{9,10... | collective-permute-start | bytes 786440 | tf_op jit(solution)/shard_map/ppermute | solution.py:34
  21.9 10.4 %copy-start.8 = (bf16[128,128]{1,0:T(8,128)(2,1)}, bf16[128,128]{1,0:T(8,128)(2,1)S(1)}, u32[]{:S(2)}) copy-start(bf16[128,128]{1,0:T(8,128)(2,1)S(1)} %collective-permute-done.r0) | copy-start | bytes 98308
  21.9 46.3 %collective-permute-start.5 = (bf16[256,512]{1,0:T(8,128)(2,1)}, bf16[256,512]{1,0:T(8,128)(2,1)S(1)}, u32[]{:S(2)}, u32[]{:S(2)}) collective-permute-start(bf16[256,512]{1,0:T(8,128)(2,1)} %get-tuple-element.38), channel_id=1, source_target_pairs={{1,0},{2,1},{3,2},{4,3},{5,4},{6,5},{7,6},{8,7},{9,8},{10,9},{11,1... | collective-permute-start | bytes 786440 | tf_op jit(solution)/shard_map/ppermute | solution.py:34
  27.0 5.4 %copy-start.9 = (bf16[128,128]{1,0:T(8,128)(2,1)}, bf16[128,128]{1,0:T(8,128)(2,1)S(1)}, u32[]{:S(2)}) copy-start(bf16[128,128]{1,0:T(8,128)(2,1)S(1)} %collective-permute-done.1.r1) | copy-start | bytes 98308
  27.0 41.3 %collective-permute-start.6 = (bf16[256,512]{1,0:T(8,128)(2,1)}, bf16[256,512]{1,0:T(8,128)(2,1)S(1)}, u32[]{:S(2)}, u32[]{:S(2)}) collective-permute-start(bf16[256,512]{1,0:T(8,128)(2,1)} %get-tuple-element.39), channel_id=1, source_target_pairs={{30,0},{31,1},{0,2},{1,3},{2,4},{3,5},{4,6},{5,7},{6,8},{7,9},{8,1... | collective-permute-start | bytes 786440 | tf_op jit(solution)/shard_map/ppermute | solution.py:34
  27.0 5.4 %copy-start.10 = (bf16[128,128]{1,0:T(8,128)(2,1)}, bf16[128,128]{1,0:T(8,128)(2,1)S(1)}, u32[]{:S(2)}) copy-start(bf16[128,128]{1,0:T(8,128)(2,1)S(1)} %collective-permute-done.2.r2) | copy-start | bytes 98308
  27.0 41.3 %collective-permute-start.7 = (bf16[256,512]{1,0:T(8,128)(2,1)}, bf16[256,512]{1,0:T(8,128)(2,1)S(1)}, u32[]{:S(2)}, u32[]{:S(2)}) collective-permute-start(bf16[256,512]{1,0:T(8,128)(2,1)} %get-tuple-element.40), channel_id=1, source_target_pairs={{2,0},{3,1},{4,2},{5,3},{6,4},{7,5},{8,6},{9,7},{10,8},{11,9},{12,... | collective-permute-start | bytes 786440 | tf_op jit(solution)/shard_map/ppermute | solution.py:34
  32.4 0.6 copy-start.11
  68.2 0.7 copy-start
  68.3 0.8 copy-start.1
  68.3 0.8 copy-start.2
  68.3 0.9 copy-start.3
  130.8 2.6 %collective-permute-start.8 = (bf16[128,128]{1,0:T(8,128)(2,1)}, bf16[128,128]{1,0:T(8,128)(2,1)S(1)}, u32[]{:S(2)}, u32[]{:S(2)}) collective-permute-start(bf16[128,128]{1,0:T(8,128)(2,1)} %get-tuple-element.44), channel_id=1, source_target_pairs={{1,0},{2,1},{3,2},{4,3},{5,4},{6,5},{7,6},{8,7},{9,8},{10,9},{11,1... | collective-permute-start | bytes 98312 | tf_op jit(solution)/shard_map/ppermute | solution.py:34
  130.9 6.9 %collective-permute-start.9 = (bf16[128,128]{1,0:T(8,128)(2,1)}, bf16[128,128]{1,0:T(8,128)(2,1)S(1)}, u32[]{:S(2)}, u32[]{:S(2)}) collective-permute-start(bf16[128,128]{1,0:T(8,128)(2,1)} %get-tuple-element.45), channel_id=1, source_target_pairs={{31,0},{0,1},{1,2},{2,3},{3,4},{4,5},{5,6},{6,7},{7,8},{8,9},{9,10... | collective-permute-start | bytes 98312 | tf_op jit(solution)/shard_map/ppermute | solution.py:34
  131.4 6.4 %collective-permute-start.10 = (bf16[128,128]{1,0:T(8,128)(2,1)}, bf16[128,128]{1,0:T(8,128)(2,1)S(1)}, u32[]{:S(2)}, u32[]{:S(2)}) collective-permute-start(bf16[128,128]{1,0:T(8,128)(2,1)} %get-tuple-element.46), channel_id=1, source_target_pairs={{2,0},{3,1},{4,2},{5,3},{6,4},{7,5},{8,6},{9,7},{10,8},{11,9},{12,... | collective-permute-start | bytes 98312 | tf_op jit(solution)/shard_map/ppermute | solution.py:34
  131.4 7.4 %collective-permute-start.11 = (bf16[128,128]{1,0:T(8,128)(2,1)}, bf16[128,128]{1,0:T(8,128)(2,1)S(1)}, u32[]{:S(2)}, u32[]{:S(2)}) collective-permute-start(bf16[128,128]{1,0:T(8,128)(2,1)} %get-tuple-element.47), channel_id=1, source_target_pairs={{30,0},{31,1},{0,2},{1,3},{2,4},{3,5},{4,6},{5,7},{6,8},{7,9},{8,1... | collective-permute-start | bytes 98312 | tf_op jit(solution)/shard_map/ppermute | solution.py:34
  133.4 5.5 %copy-start.4 = (bf16[128,128]{1,0:T(8,128)(2,1)}, bf16[128,128]{1,0:T(8,128)(2,1)S(1)}, u32[]{:S(2)}) copy-start(bf16[128,128]{1,0:T(8,128)(2,1)S(1)} %collective-permute-done.8.b0) | copy-start | bytes 98308
  137.8 1.0 copy-start.5
  137.8 1.0 copy-start.6
  138.9 0.6 copy-start.7

commit v2 on v1

v2 whole, which is shorter than its diff:
```python
import functools
import math

import jax
import jax.numpy as jnp
from jax import lax
from jax.experimental import pallas as pl
from jax.experimental.pallas import tpu as pltpu
from jax.sharding import PartitionSpec as P

INV_ROOT = 0.7071067811865476
BF = jnp.bfloat16
F32 = jnp.float32
MESH = pl.DeviceIdType.MESH
VMEM_LIMIT = 56 * 1024 * 1024

E = 1024
K = 32
B = 112
TW = 64
D = 512
CAP = 256
NL = 4
G = 8
T = G * K


def offsets(count):
    return [(which // 2 + 1) * (1 - 2 * (which % 2)) for which in range(count)]


def sigmoid(v):
    return 1.0 / (1.0 + jnp.exp(-v))


def silu(v):
    return v * sigmoid(v)


def slope(v):
    s = sigmoid(v)
    return s * (1.0 + v * (1.0 - s))


def iota(shape, dim):
    return lax.broadcasted_iota(jnp.int32, shape, dim)


def dot(a, b):
    return jnp.dot(a, b, preferred_element_type=F32)


def dot_nt(a, b):
    return lax.dot_general(a, b, (((1,), (1,)), ((), ())), preferred_element_type=F32)


def dot_tn(a, b):
    return lax.dot_general(a, b, (((0,), (0,)), ((), ())), preferred_element_type=F32)


def onehot(cond):
    return jnp.where(cond, 1.0, 0.0).astype(BF)


GS = 8
GP = 4
STEPS = E // (G * GS)


def graph_at(distance):
    n = lax.axis_size("graph")
    return (lax.axis_index("dp"), lax.rem(lax.axis_index("graph") + (distance + n), n))


def remote(src, dst, send, recv, where):
    return pltpu.make_async_remote_copy(
        src, dst, send, recv, device_id=where, device_id_type=MESH
    )


def greet(where):
    pl.semaphore_signal(
        pltpu.get_barrier_semaphore(), inc=1, device_id=where, device_id_type=MESH
    )


def load_w(wp, w_bil):
    wp[...] = jnp.zeros_like(wp)
    for ch in range(16):
        wp[128 * ch : 128 * ch + B, :] = w_bil[:, 256 * ch : 256 * ch + 256]


def fold(rows):
    half = rows.shape[0] // 2
    return jnp.concatenate([rows[:half], rows[half:]], axis=1)


def unfold(rows):
    return jnp.concatenate([rows[:, :TW], rows[:, TW:]], axis=0)


def fwd_kernel(msg, cot, w_edge, w_down, rows, count, basis, idx, w_bil, outer, bas, state, cot_out,
               red, pool_t, wp, sbuf, red_send, red_recv, cot_send, cot_recv, send, recv):
    step = pl.program_id(0)
    shifts = offsets(NL)

    def red_copy(o):
        where = graph_at(shifts[o])
        return remote(red_send.at[o], red_recv.at[o], send.at[0, o], recv.at[0, o], where)

    def cot_copy(o):
        where = graph_at(shifts[o])
        return remote(cot_send.at[o], cot_recv.at[o], send.at[1, o], recv.at[1, o], where)

    @pl.when(step == 0)
    def _():
        for o in range(NL):
            greet(graph_at(shifts[o]))
        for i in range(4):
            m = pl.ds(256 * i, 256)
            hidden = silu(dot(msg[m, :], w_edge[...])).astype(BF)
            red[m, :] = silu(dot_nt(hidden, w_down[...])).astype(BF)
        lane = iota((1, CAP), 1)
        lists = []
        for o in range(NL):
            lists.append(jnp.where(lane < count[0, o], rows[o : o + 1, :], -1))
        picks = jnp.concatenate(lists + lists, axis=0).T
        wide = iota((CAP, E), 1)
        for o in range(NL):
            red_send[o] = fold(dot(onehot(wide == picks[:, o : o + 1]), red[...]).astype(BF))
        pl.semaphore_wait(pltpu.get_barrier_semaphore(), NL)
        for o in range(NL):
            red_copy(o).start()
        for o in range(NL):
            cot_send[o] = dot(onehot(wide == picks[:, o : o + 1]), cot[...]).astype(BF)
            cot_copy(o).start()
        load_w(wp, w_bil)
        for hi in range(8):
            if hi < 4:
                src = fold(red[256 * hi : 256 * hi + 256, :])
            else:
                red_copy(hi - 4).wait_recv()
                src = red_recv[hi - 4]
            flip = src.astype(F32).T
            pool_t[64 * hi : 64 * hi + 64, :] = jnp.concatenate(
                [flip[:64], flip[64:]], axis=1
            ).astype(BF)

    @pl.when(step == STEPS - 1)
    def _():
        for o in range(NL):
            red_copy(o).wait_send()
            cot_copy(o).wait()
        cot_out[...] = cot_recv[...]

    e_lane = lax.rem(iota((16, T), 1), G)
    quad = iota((16, T), 0) // 4
    keep = [onehot(e_lane == 4 * q + quad) for q in range(2)]
    low = iota((8, T), 0) < 4

    def some(j, carry):
        hots, his = [], []
        for i in range(GP):
            row = idx[pl.ds(j * GP + i, 1), :]
            hots.append(onehot(iota((256, T), 0) == jnp.bitwise_and(row, 255)))
            his.append(jnp.right_shift(row, 8))
        found = dot(pool_t[...], jnp.concatenate(hots, axis=1))
        for i in range(GP):
            g = j * GP + i
            wide = basis[pl.ds(pl.multiple_of(g * G, G), G), :].astype(F32)
            pieces = []
            for k in range(K):
                piece = wide[:, k * B : (k + 1) * B]
                pieces.append(jnp.concatenate([piece, jnp.zeros((G, 128 - B), F32)], axis=1))
            rhs = jnp.concatenate(pieces, axis=0).astype(BF)
            bas[pl.ds(pl.multiple_of(g * T, T), T), :] = rhs
            got = jnp.zeros((TW, T), F32)
            for hi in range(8):
                part = found[64 * hi : 64 * hi + 64, T * i : T * i + T]
                got = jnp.where(his[i] == hi, part, got)
            tiles = []
            for v in range(8):
                x = got[8 * v : 8 * v + 8]
                y = pltpu.roll(x, 4, 0)
                for d in (jnp.where(low, x, y), jnp.where(low, y, x)):
                    tiles.append(jnp.concatenate([d, d], axis=0).astype(BF))
            lhs = jnp.concatenate([t * keep[q] for q in range(2) for t in tiles], axis=0)
            out = dot(lhs, rhs).astype(BF)
            for q in range(2):
                for ch in range(16):
                    at = (q * 16 + ch) * 16
                    outer[pl.ds(pl.multiple_of(g * 32 + 16 * q, 16), 16), 128 * ch : 128 * ch + 128] = (
                        out[at : at + 16]
                    )
        return carry

    lax.fori_loop(0, GS // GP, some, 0)
    rows = 32 * GS
    full = dot(outer[...], wp[...])
    full = jnp.where(lax.rem(iota((rows, 256), 0), 4) == iota((rows, 256), 1) // 64, full, 0.0)
    full = full + pltpu.roll(full, 1, 0)
    full = full + pltpu.roll(full, 2, 0)
    sbuf[...] = full[:, :128] + full[:, 128:]
    picked = sbuf[pl.ds(3, G * GS, stride=4), :]
    state[...] = (picked + pltpu.roll(picked, 64, 1)).astype(BF)


def fwd(msg, cot, w_edge, w_down, rows, count, basis, idx, w_bil):
    whole = lambda shape: pl.BlockSpec(shape, lambda i: (0,) * len(shape))
    return pl.pallas_call(
        fwd_kernel,
        grid=(STEPS,),
        out_shape=[
            jax.ShapeDtypeStruct((4 * E, 2048), BF),
            jax.ShapeDtypeStruct((E * K, 128), BF),
            jax.ShapeDtypeStruct((E, 128), BF),
            jax.ShapeDtypeStruct((NL, CAP, D), BF),
        ],
        in_specs=[
            whole((E, D)), whole((E, D)), whole((D, D)), whole((TW, D)), whole((NL, CAP)),
            pl.BlockSpec(memory_space=pltpu.SMEM),
            pl.BlockSpec((G * GS, K * B), lambda i: (i, 0)),
            pl.BlockSpec((GS, T), lambda i: (i, 0)),
            whole((B, 4096)),
        ],
        out_specs=[
            pl.BlockSpec((32 * GS, 2048), lambda i: (i, 0)),
            pl.BlockSpec((T * GS, 128), lambda i: (i, 0)),
            pl.BlockSpec((G * GS, 128), lambda i: (i, 0)),
            whole((NL, CAP, D)),
        ],
        scratch_shapes=[
            pltpu.VMEM((E, TW), BF),
            pltpu.VMEM((512, 256), BF),
            pltpu.VMEM((2048, 256), BF),
            pltpu.VMEM((32 * GS, 128), F32),
            pltpu.VMEM((NL, 128, 128), BF),
            pltpu.VMEM((NL, 128, 128), BF),
            pltpu.VMEM((NL, CAP, D), BF),
            pltpu.VMEM((NL, CAP, D), BF),
            pltpu.SemaphoreType.DMA((2, NL)),
            pltpu.SemaphoreType.DMA((2, NL)),
        ],
        compiler_params=pltpu.CompilerParams(
            collective_id=0, has_side_effects=True, vmem_limit_bytes=VMEM_LIMIT
        ),
        name="triplets_out",
    )(msg, cot, w_edge, w_down, rows, count, basis, idx, w_bil)


BE = 128


def mid_kernel(factor, state, outer, cot, all_cot, far_cot, rev, w_up, count, gsx, early, bil, up):
    step = pl.program_id(0)

    @pl.when(step == 0)
    def _():
        bil[...] = jnp.zeros_like(bil)
        up[...] = jnp.zeros_like(up)

    st = state[...][:, :TW]
    alive = iota((BE, D), 0) + step * BE < count[0, 0]
    scaled = jnp.where(alive, cot[...].astype(F32) * INV_ROOT, 0.0)
    grad_ca = (scaled * slope(dot(st, w_up[0]))).astype(BF)
    row = rev[pl.ds(step, 1), :]
    col = jnp.concatenate([row] * 8, axis=0).T[:, :1]
    mirror = dot(onehot(iota((BE, E), 1) == col), all_cot[...])
    mirror = mirror + dot(onehot(iota((BE, NL * CAP), 1) + E == col), far_cot[...])
    grad_ac = (mirror * INV_ROOT * slope(dot(st, w_up[1]))).astype(BF)
    up[:TW, :] += dot_tn(st, grad_ca)
    up[TW:, :] += dot_tn(st, grad_ac)
    own = dot_nt(grad_ca, jnp.concatenate([w_up[0]] * 4, axis=0))
    back = dot_nt(grad_ac, jnp.concatenate([w_up[1]] * 4, axis=0)).astype(BF)
    grad_state = (own + back.astype(F32)).astype(BF)
    spread = onehot(iota((4 * BE, BE), 0) // 4 == iota((4 * BE, BE), 1))
    big = dot(spread, grad_state)
    big = jnp.where(lax.rem(iota((4 * BE, 256), 0), 4) == iota((4 * BE, 256), 1) // 64, big, 0.0)
    big = big.astype(BF)
    gsx[...] = big
    bil[...] += dot_tn(big, outer[...])

    @pl.when(step == pl.num_programs(0) - 1)
    def _():
        turned = (up[...] * factor).T.astype(BF)
        for i in range(32):
            early[i, :, 1024:1152] = turned[16 * i : 16 * i + 16]
            r, c = (i % 2) * 128, (i // 2) * 128
            for j in range(8):
                early[i, :, 128 * j : 128 * j + 128] = (
                    bil[r + 16 * j : r + 16 * j + 16, c : c + 128] * factor
                ).astype(BF)


def mid(factor, state, outer, cot, recv, rev, w_up, count):
    whole = lambda shape: pl.BlockSpec(shape, lambda i: (0,) * len(shape))
    return pl.pallas_call(
        functools.partial(mid_kernel, factor),
        grid=(E // BE,),
        out_shape=[
            jax.ShapeDtypeStruct((4 * E, 256), BF),
            jax.ShapeDtypeStruct((32, 16, 1152), BF),
        ],
        in_specs=[
            pl.BlockSpec((BE, 128), lambda i: (i, 0)),
            pl.BlockSpec((4 * BE, 2048), lambda i: (i, 0)),
            pl.BlockSpec((BE, D), lambda i: (i, 0)),
            whole((E, D)),
            whole((NL * CAP, D)),
        ]
        + [whole((8, 128)), whole((2, TW, D)), pl.BlockSpec(memory_space=pltpu.SMEM)],
        out_specs=[
            pl.BlockSpec((4 * BE, 256), lambda i: (i, 0)),
            whole((32, 16, 1152)),
        ],
        scratch_shapes=[pltpu.VMEM((256, 2048), F32), pltpu.VMEM((2 * TW, D), F32)],
        compiler_params=pltpu.CompilerParams(vmem_limit_bytes=VMEM_LIMIT),
        name="middle",
    )(state, outer, cot, cot, recv, rev, w_up, count)


SWAP = 10


def bwd_kernel(factor, n, n_dp, gsx, bas, idx, w_bil, early, msg, w_edge, w_down, rows, count,
               grad_msg, sum_e, sum_l, wp, go, acc, ret_send, ret_recv, s_edge, hid, s_down, gedge,
               late, in_e, pair_in, pair_out, in_l, dp_e, dp_l,
               e_send, e_recv, l_send, l_recv, r_send, r_recv, p_send, p_recv, d_send, d_recv):
    step = pl.program_id(0)
    shifts = offsets(NL)
    me = lax.axis_index("graph")
    dp = lax.axis_index("dp")
    core = lax.rem(me, 2)
    chip = me // 2
    chips = n // 2

    def early_copy(d):
        to = lax.rem(me + d, n)
        return remote(early.at[to], in_e.at[d], e_send.at[d], e_recv.at[d], (dp, to))

    def late_copy(d):
        to = lax.rem(chip + d, chips)
        return remote(pair_out.at[to], in_l.at[d], l_send.at[d], l_recv.at[d], (dp, 2 * to + core))

    def swap(which, buf):
        out = []
        for d in range(1, n_dp):
            where = (lax.rem(dp + d, n_dp), me)
            out.append(remote(buf.at[0], buf.at[d], d_send.at[which, d], d_recv.at[which, d], where))
        return out

    def total(buf):
        terms = [buf[d].astype(F32) for d in range(n_dp)]
        out = jnp.zeros_like(terms[0])
        for source in range(n_dp):
            for d in range(n_dp):
                hit = lax.rem(dp + (n_dp - d), n_dp) == source
                out = out + jnp.where(hit, terms[d], 0.0)
        return out

    @pl.when(step == 0)
    def _():
        def hello(d, carry):
            greet((dp, lax.rem(me + d, n)))
            return carry

        lax.fori_loop(1, n, hello, 0)
        for d in range(1, n_dp):
            greet((lax.rem(dp + d, n_dp), me))
        load_w(wp, w_bil)
        acc[...] = jnp.zeros_like(acc)
        pl.semaphore_wait(pltpu.get_barrier_semaphore(), n - 1 + n_dp - 1)

        def begin(d, carry):
            early_copy(d).start()
            return carry

        lax.fori_loop(1, n, begin, 0)

    @pl.when(step == SWAP)
    def _():
        def take(d, total_):
            early_copy(d).wait()
            return total_ + in_e[d].astype(F32)

        dp_e[0] = lax.fori_loop(1, n, take, early[me].astype(F32)).astype(BF)
        for c in swap(0, dp_e):
            c.start()

    go[...] = dot_nt(gsx[...], wp[...]).astype(BF)
    e_lane = lax.rem(iota((8, T), 1), G)
    pair = e_lane // 2
    odd = lax.rem(e_lane, 2) == 1
    stay = (iota((8, T), 0) >= 4) == odd

    def some(j, carry):
        hots, sides = [], []
        for i in range(GP):
            g = j * GP + i
            row = idx[pl.ds(g, 1), :]
            hots.append(onehot(iota((256, T), 0) == jnp.bitwise_and(row, 255)))
            hi_of = jnp.right_shift(row, 8)
            lhs = jnp.concatenate(
                [
                    go[pl.ds(pl.multiple_of(g * 32 + 16 * q, 16), 16), 128 * ch : 128 * ch + 128]
                    for q in range(2)
                    for ch in range(16)
                ],
                axis=0,
            )
            full = dot_nt(lhs, bas[pl.ds(pl.multiple_of(g * T, T), T), :])
            picked = []
            for ch in range(16):
                z = full[16 * ch : 16 * ch + 8]
                for p in range(1, 4):
                    at = (p // 2) * 256 + 16 * ch + 8 * (p % 2)
                    z = jnp.where(pair == p, full[at : at + 8], z)
                picked.append(z)
            grads = []
            for v in range(8):
                z0, z1 = picked[2 * v], picked[2 * v + 1]
                here = jnp.where(odd, z1, z0)
                there = jnp.where(odd, z0, z1)
                grads.append(jnp.where(stay, here, pltpu.roll(there, 4, 0)))
            grad = jnp.concatenate(grads, axis=0).astype(BF)
            sides.append(
                jnp.concatenate([grad * onehot(hi_of == hi) for hi in range(8)], axis=0)
            )
        acc[...] += dot_nt(jnp.concatenate(sides, axis=1), jnp.concatenate(hots, axis=1))
        return carry

    lax.fori_loop(0, GS // GP, some, 0)

    @pl.when(step == pl.num_programs(0) - 1)
    def _():
        def back(o):
            return remote(ret_send.at[o], ret_recv.at[o], r_send.at[o], r_recv.at[o], graph_at(-shifts[o]))

        for o in range(NL):
            part = acc[64 * (4 + o) : 64 * (4 + o) + 64, :]
            ret_send[o] = jnp.concatenate([part[:, :128], part[:, 128:]], axis=0).T.astype(BF)
            back(o).start()
        for i in range(4):
            m = pl.ds(256 * i, 256)
            pre_edge = dot(msg[m, :], w_edge[...])
            s_edge[m, :] = slope(pre_edge)
            hidden = silu(pre_edge).astype(BF)
            hid[m, :] = hidden
            s_down[m, :] = slope(dot_nt(hidden, w_down[...]))
        hots, backs = [], []
        for o in range(NL):
            picks = jnp.where(iota((1, CAP), 1) < count[0, o], rows[o : o + 1, :], -1)
            hots.append(onehot(iota((E, CAP), 0) == picks))
        for o in range(NL):
            back(o).wait()
            backs.append(unfold(ret_recv[o]))
        far = dot(jnp.concatenate(hots, axis=1), jnp.concatenate(backs, axis=0))
        downs = jnp.zeros((D, TW), F32)
        for i in range(4):
            m = pl.ds(256 * i, 256)
            part = acc[64 * i : 64 * i + 64, :]
            own = jnp.concatenate([part[:, :128], part[:, 128:]], axis=0).T
            grad_down = ((far[256 * i : 256 * i + 256] + unfold(own)) * s_down[m, :]).astype(BF)
            downs = downs + dot_tn(hid[m, :], grad_down)
            gedge[m, :] = (dot(grad_down, w_down[...]) * s_edge[m, :]).astype(BF)
        edges = dot_tn(msg[...], gedge[...])
        both = jnp.concatenate(
            [edges * factor, downs * factor, jnp.zeros((D, TW), F32)], axis=1
        ).astype(BF)
        for i in range(n):
            late[i % 2, i // 2] = both[16 * i : 16 * i + 16]
        sibling = (dp, me + 1 - 2 * core)
        first = remote(late.at[1 - core], pair_in, p_send, p_recv, sibling)
        first.start()
        for i in range(4):
            m = pl.ds(256 * i, 256)
            grad_msg[m, :] = dot_nt(gedge[m, :], w_edge[...]).astype(BF)
        first.wait()
        pair_out[...] = (late[core].astype(F32) + pair_in[...].astype(F32)).astype(BF)

        def begin(d, carry):
            late_copy(d).start()
            return carry

        lax.fori_loop(1, chips, begin, 0)
        for c in swap(0, dp_e):
            c.wait()
        sum_e[...] = total(dp_e)

        def take(d, total_):
            late_copy(d).wait()
            return total_ + in_l[d].astype(F32)

        dp_l[0] = lax.fori_loop(1, chips, take, pair_out[chip].astype(F32)).astype(BF)
        for c in swap(1, dp_l):
            c.start()
        for c in swap(1, dp_l):
            c.wait()
        sum_l[...] = total(dp_l)


def bwd(factor, gsx, bas, idx, w_bil, early, msg, w_edge, w_down, rows, count):
    whole = lambda shape: pl.BlockSpec(shape, lambda i: (0,) * len(shape))
    n = lax.axis_size("graph")
    n_dp = lax.axis_size("dp")
    dma = pltpu.SemaphoreType.DMA
    return pl.pallas_call(
        functools.partial(bwd_kernel, factor, n, n_dp),
        grid=(STEPS,),
        out_shape=[
            jax.ShapeDtypeStruct((E, D), BF),
            jax.ShapeDtypeStruct((16, 1152), F32),
            jax.ShapeDtypeStruct((16, 640), F32),
        ],
        in_specs=[
            pl.BlockSpec((32 * GS, 256), lambda i: (i, 0)),
            pl.BlockSpec((T * GS, 128), lambda i: (i, 0)),
            pl.BlockSpec((GS, T), lambda i: (i, 0)),
            whole((B, 4096)), whole((n, 16, 1152)),
            whole((E, D)), whole((D, D)), whole((TW, D)), whole((NL, CAP)),
            pl.BlockSpec(memory_space=pltpu.SMEM),
        ],
        out_specs=[whole((E, D)), whole((16, 1152)), whole((16, 640))],
        scratch_shapes=[
            pltpu.VMEM((2048, 256), BF),
            pltpu.VMEM((32 * GS, 2048), BF),
            pltpu.VMEM((512, 256), F32),
            pltpu.VMEM((NL, 128, 128), BF),
            pltpu.VMEM((NL, 128, 128), BF),
            pltpu.VMEM((E, D), F32),
            pltpu.VMEM((E, D), BF),
            pltpu.VMEM((E, TW), F32),
            pltpu.VMEM((E, D), BF),
            pltpu.VMEM((2, n // 2, 16, 640), BF),
            pltpu.VMEM((n, 16, 1152), BF),
            pltpu.VMEM((n // 2, 16, 640), BF),
            pltpu.VMEM((n // 2, 16, 640), BF),
            pltpu.VMEM((n // 2, 16, 640), BF),
            pltpu.VMEM((n_dp, 16, 1152), BF),
            pltpu.VMEM((n_dp, 16, 640), BF),
            dma((n,)), dma((n,)), dma((n // 2,)), dma((n // 2,)), dma((NL,)), dma((NL,)),
            dma, dma, dma((2, n_dp)), dma((2, n_dp)),
        ],
        compiler_params=pltpu.CompilerParams(
            collective_id=1, has_side_effects=True, vmem_limit_bytes=VMEM_LIMIT
        ),
        name="triplets_back",
    )(gsx, bas, idx, w_bil, early, msg, w_edge, w_down, rows, count)


def last_kernel(grad_msg, e, l, o_msg, o_edge, o_down, o_bil, o_up, sem):
    move = pltpu.make_async_copy(grad_msg, o_msg, sem)
    move.start()
    o_edge[...] = l[:, :D]
    o_down[...] = l[:, D : D + TW]
    square = jnp.concatenate([e[:, 128 * j : 128 * j + 128] for j in range(8)], axis=0).T
    o_bil[...] = square[:B]
    o_up[0] = e[:, 1024:1088]
    o_up[1] = e[:, 1088:1152]
    move.wait()


def last(grad_msg, e, l):
    vm = pl.BlockSpec(memory_space=pltpu.VMEM)
    hbm = pl.BlockSpec(memory_space=pl.ANY)
    return pl.pallas_call(
        last_kernel,
        out_shape=[
            jax.ShapeDtypeStruct((E, D), BF),
            jax.ShapeDtypeStruct((16, D), F32),
            jax.ShapeDtypeStruct((16, TW), F32),
            jax.ShapeDtypeStruct((B, 128), F32),
            jax.ShapeDtypeStruct((2, 16, TW), F32),
        ],
        in_specs=[hbm, vm, vm],
        out_specs=[hbm, vm, vm, vm, vm],
        scratch_shapes=[pltpu.SemaphoreType.DMA],
        name="outputs",
    )(grad_msg, e, l)


def body(
    messages, cotangent, triplet_basis, w_edge, w_down, w_bil, w_up,
    trip_src, send_rows, send_count, rev_src, edge_count,
):
    msg, cot = messages[0], cotangent[0]
    narrow = w_down.T
    rows = send_rows[0]
    factor = 1.0 / math.sqrt(lax.axis_size("dp") * lax.axis_size("graph") * E)
    idx = trip_src[0].reshape(E // G, G, K).transpose(0, 2, 1).reshape(E // G, T)
    outer, bas, state, far = fwd(
        msg, cot, w_edge, narrow, rows, send_count, triplet_basis[0], idx, w_bil
    )
    gsx, early = mid(
        factor, state, outer, cot, far.reshape(NL * CAP, D), rev_src.reshape(8, 128), w_up, edge_count
    )
    grad_msg, e, l = bwd(factor, gsx, bas, idx, w_bil, early, msg, w_edge, narrow, rows, send_count)
    grad_msg, g_edge, g_down, g_bil, g_up = last(grad_msg, e, l)
    return grad_msg[None], g_edge, g_down, g_bil, g_up.transpose(0, 2, 1)


def solution(mesh):
    row = P("dp", "graph", None)
    flat = P("dp", "graph")
    return jax.shard_map(
        body,
        mesh=mesh,
        in_specs=(row, row, row, P(), P(), P(), P(), row, row, flat, flat, flat),
        out_specs=(
            row,
            P("graph", None),
            P("graph", None),
            P(None, "graph"),
            P(None, None, "graph"),
        ),
        check_vma=False,
    )
```

time: 197 us -> 173 us (0.88)
  starting transfers between devices: 24.1 us -> 0 us
  Pallas kernels: 153 us -> 169 us
  local copies, waits for them, and re-layouts: 11.4 us -> 2.08 us
  waiting for transfers between devices: 5.47 us -> 0 us
    ppermute x12 -> x0, starting transfers between devices: 24.1 us -> none  [shifted(): lax.ppermute(block, axis, [((i - distance) % n, i) for i in range(n)])]
    pallas_call x1, Pallas kernels: 35.3 us -> 47.5 us  [fwd(): pl.pallas_call(fwd_kernel, grid=(STEPS,), out_shape=[jax.ShapeDtypeStruct...]
    unnamed x30 -> x1, local copies, waits for them, and re-layouts: 10.4 us -> 1.1 us
    ppermute x12 -> x0, waiting for transfers between devices: 5.47 us -> none  [shifted(): lax.ppermute(block, axis, [((i - distance) % n, i) for i in range(n)])]
    pallas_call x4 -> x2, Pallas kernels: 97.1 us -> 101 us  [the longest x1 66.5 us: bwd(): pl.pallas_call(functools.partial(bwd_kernel, factor, n, n_dp), grid=(STEP...]
  transfers between devices with their start and end apart: 12 -> 0, of which waited for: 2 -> 0; matrix products, arithmetic and copies ran while one was open for 1% -> 0% of each run, Pallas kernels for 18% -> 0%
where the time goes in v2:
time: 173 us
  Pallas kernels  169 us (98%)
  local copies, waits for them, and re-layouts  2.08 us (1%)
    pallas_call x1, Pallas kernels, bwd(): pl.pallas_call(functools.partial(bwd_kernel, factor, n, n_dp), grid=(STEP...  66.5 us
    pallas_call x1, Pallas kernels, fwd(): pl.pallas_call(fwd_kernel, grid=(STEPS,), out_shape=[jax.ShapeDtypeStruct...  47.5 us
    pallas_call x1, Pallas kernels, last(): pl.pallas_call(last_kernel, out_shape=[jax.ShapeDtypeStruct((E, D), BF),...  34.4 us
    pallas_call x1, Pallas kernels, mid(): pl.pallas_call(functools.partial(mid_kernel, factor), grid=(E // BE,), ou...  20.8 us

profile of v2, /device:TPU:0, one launch (start us, length us, event | category | flops | bytes accessed | tf_op | source)
XLA Modules:
  0.0 172.8 jit_solution(9315383708060813311)
XLA Ops:
  1.3 1.1 copy.18
  2.4 0.2 copy.19
  2.6 0.8 copy.20.idx
  3.4 47.5 %triplets_out.1 = (bf16[4096,2048]{1,0:T(8,128)(2,1)}, bf16[32768,128]{1,0:T(8,128)(2,1)}, bf16[1024,128]{1,0:T(8,128)(2,1)}, bf16[4,256,512]{2,1,0:T(8,128)(2,1)}) custom-call(bf16[1024,512]{1,0:T(8,128)(2,1)} %bitcast.17, bf16[1024,512]{1,0:T(8,128)(2,1)} %bitcast.13, bf16[512,512]{1,0:T(8,128)(2,1)} %w_edge.3, bf16[64,512]{1,0:T(8,128)(2,1)} %bitcast.22, ...), custom_call_target="tpu_custom_call" | custom-call | tf_op jit(solution)/shard_map/triplets_out/pallas_call | solution.py:210
  50.9 20.8 %middle.1 = (bf16[4096,256]{1,0:T(8,128)(2,1)}, bf16[32,16,1152]{2,1,0:T(8,128)(2,1)}) custom-call(bf16[1024,128]{1,0:T(8,128)(2,1)} %get-tuple-element.19.state, bf16[4096,2048]{1,0:T(8,128)(2,1)} %get-tuple-element.20.outer, bf16[1024,512]{1,0:T(8,128)(2,1)} %bitcast.14, bf16[1024,512]{1,0:T(8,128)(2,1)} %bitcast.15, bf16[1024,512]{1,0:T(8,128)(2,1)} %bitcast.20, ...), custom_call_target="tpu_custom_call" | custom-call | tf_op jit(solution)/shard_map/middle/pallas_call | solution.py:297
  71.7 66.5 %triplets_back.1 = (bf16[1024,512]{1,0:T(8,128)(2,1)}, f32[16,1152]{1,0:T(8,128)}, f32[16,640]{1,0:T(8,128)}) custom-call(bf16[4096,256]{1,0:T(8,128)(2,1)} %get-tuple-element.22.gsx, bf16[32768,128]{1,0:T(8,128)(2,1)} %get-tuple-element.23.bas, s32[128,256]{1,0:T(8,128)} %copy.20.idx, bf16[112,4096]{1,0:T(8,128)(2,1)} %w_bil.3, ...), custom_call_target="tpu_custom_call" | custom-call | tf_op jit(solution)/shard_map/triplets_back/pallas_call | solution.py:507
  138.2 34.4 %outputs.1 = (bf16[1024,512]{1,0:T(8,128)(2,1)}, f32[16,512]{1,0:T(8,128)}, f32[16,64]{1,0:T(8,128)}, f32[112,128]{1,0:T(8,128)}, f32[2,16,64]{2,1,0:T(8,128)}) custom-call(bf16[1024,512]{1,0:T(8,128)(2,1)} %get-tuple-element.25.grad_msg, f32[16,1152]{1,0:T(8,128)} %get-tuple-element.26.e, f32[16,640]{1,0:T(8,128)} %get-tuple-element.27.l), custom_call_target="tpu_custom_call" | custom-call | tf_op jit(solution)/shard_map/outputs/pallas_call | solution.py:566

commit v3 on v2

--- a/solution.py
+++ b/solution.py
@@ -30,7 +30,7 @@
 
 
 def sigmoid(v):
-    return 1.0 / (1.0 + jnp.exp(-v))
+    return 0.5 + 0.5 * jnp.tanh(0.5 * v)
 
 
 def silu(v):
@@ -62,7 +62,7 @@
     return jnp.where(cond, 1.0, 0.0).astype(BF)
 
 
-GS = 8
+GS = 16
 GP = 4
 STEPS = E // (G * GS)
 
@@ -153,10 +153,9 @@
             cot_copy(o).wait()
         cot_out[...] = cot_recv[...]
 
-    e_lane = lax.rem(iota((16, T), 1), G)
-    quad = iota((16, T), 0) // 4
-    keep = [onehot(e_lane == 4 * q + quad) for q in range(2)]
+    keep = onehot(lax.rem(iota((16, T), 1), 4) == iota((16, T), 0) // 4)
     low = iota((8, T), 0) < 4
+    low1 = iota((8, 128), 0) < 4
 
     def some(j, carry):
         hots, his = [], []
@@ -164,7 +163,8 @@
             row = idx[pl.ds(j * GP + i, 1), :]
             hots.append(onehot(iota((256, T), 0) == jnp.bitwise_and(row, 255)))
             his.append(jnp.right_shift(row, 8))
-        found = dot(pool_t[...], jnp.concatenate(hots, axis=1))
+        found = dot(pool_t[...], jnp.concatenate(hots, axis=1)).astype(BF)
+        founds = [found[:, T * i : T * i + T] for i in range(GP)]
         for i in range(GP):
             g = j * GP + i
             wide = basis[pl.ds(pl.multiple_of(g * G, G), G), :].astype(F32)
@@ -172,25 +172,37 @@
             for k in range(K):
                 piece = wide[:, k * B : (k + 1) * B]
                 pieces.append(jnp.concatenate([piece, jnp.zeros((G, 128 - B), F32)], axis=1))
-            rhs = jnp.concatenate(pieces, axis=0).astype(BF)
-            bas[pl.ds(pl.multiple_of(g * T, T), T), :] = rhs
-            got = jnp.zeros((TW, T), F32)
-            for hi in range(8):
-                part = found[64 * hi : 64 * hi + 64, T * i : T * i + T]
-                got = jnp.where(his[i] == hi, part, got)
+            first, second = [], []
+            for k in range(0, K, 2):
+                x, y = pieces[k], pieces[k + 1]
+                z = pltpu.roll(jnp.where(low1, y, x), 4, 0)
+                first.append(jnp.where(low1, x, z))
+                second.append(jnp.where(low1, z, y))
+            first = jnp.concatenate(first, axis=0).astype(BF)
+            second = jnp.concatenate(second, axis=0).astype(BF)
+            zero = jnp.zeros((128, 128), BF)
+            at = pl.multiple_of(g * T, T)
+            bas[pl.ds(at, 128), :] = first
+            bas[pl.ds(at + 128, 128), :] = second
+            rhs = jnp.concatenate(
+                [jnp.concatenate([first, zero], axis=1), jnp.concatenate([zero, second], axis=1)], axis=0
+            )
+            got = founds[i][:64] * onehot(his[i] == 0)
+            for hi in range(1, 8):
+                got = got + founds[i][64 * hi : 64 * hi + 64] * onehot(his[i] == hi)
+            got = got.astype(F32)
             tiles = []
             for v in range(8):
                 x = got[8 * v : 8 * v + 8]
                 y = pltpu.roll(x, 4, 0)
                 for d in (jnp.where(low, x, y), jnp.where(low, y, x)):
-                    tiles.append(jnp.concatenate([d, d], axis=0).astype(BF))
-            lhs = jnp.concatenate([t * keep[q] for q in range(2) for t in tiles], axis=0)
+                    tiles.append(jnp.concatenate([d, d], axis=0).astype(BF) * keep)
+            lhs = jnp.concatenate(tiles, axis=0)
             out = dot(lhs, rhs).astype(BF)
             for q in range(2):
                 for ch in range(16):
-                    at = (q * 16 + ch) * 16
                     outer[pl.ds(pl.multiple_of(g * 32 + 16 * q, 16), 16), 128 * ch : 128 * ch + 128] = (
-                        out[at : at + 16]
+                        out[16 * ch : 16 * ch + 16, 128 * q : 128 * q + 128]
                     )
         return carry
 
@@ -319,7 +331,7 @@
     )(state, outer, cot, cot, recv, rev, w_up, count)
 
 
-SWAP = 10
+SWAP = 5
 
 
 def bwd_kernel(factor, n, n_dp, gsx, bas, idx, w_bil, early, msg, w_edge, w_down, rows, count,
@@ -388,8 +400,8 @@
             c.start()
 
     go[...] = dot_nt(gsx[...], wp[...]).astype(BF)
-    e_lane = lax.rem(iota((8, T), 1), G)
-    pair = e_lane // 2
+    e_lane = lax.rem(iota((8, T), 1), 4)
+    upper = e_lane >= 2
     odd = lax.rem(e_lane, 2) == 1
     stay = (iota((8, T), 0) >= 4) == odd
 
@@ -402,20 +414,31 @@
             hi_of = jnp.right_shift(row, 8)
             lhs = jnp.concatenate(
                 [
-                    go[pl.ds(pl.multiple_of(g * 32 + 16 * q, 16), 16), 128 * ch : 128 * ch + 128]
-                    for q in range(2)
+                    jnp.concatenate(
+                        [
+                            go[pl.ds(pl.multiple_of(g * 32 + 16 * q, 16), 16), 128 * ch : 128 * ch + 128]
+                            for q in range(2)
+                        ],
+                        axis=1,
+                    )
                     for ch in range(16)
                 ],
                 axis=0,
             )
-            full = dot_nt(lhs, bas[pl.ds(pl.multiple_of(g * T, T), T), :])
-            picked = []
-            for ch in range(16):
-                z = full[16 * ch : 16 * ch + 8]
-                for p in range(1, 4):
-                    at = (p // 2) * 256 + 16 * ch + 8 * (p % 2)
-                    z = jnp.where(pair == p, full[at : at + 8], z)
-                picked.append(z)
+            at = pl.multiple_of(g * T, T)
+            zero = jnp.zeros((128, 128), BF)
+            side = jnp.concatenate(
+                [
+                    jnp.concatenate([bas[pl.ds(at, 128), :], zero], axis=1),
+                    jnp.concatenate([zero, bas[pl.ds(at + 128, 128), :]], axis=1),
+                ],
+                axis=0,
+            )
+            full = dot_nt(lhs, side)
+            picked = [
+                jnp.where(upper, full[16 * ch + 8 : 16 * ch + 16], full[16 * ch : 16 * ch + 8])
+                for ch in range(16)
+            ]
             grads = []
             for v in range(8):
                 z0, z1 = picked[2 * v], picked[2 * v + 1]
@@ -548,23 +571,25 @@
     )(gsx, bas, idx, w_bil, early, msg, w_edge, w_down, rows, count)
 
 
-def last_kernel(grad_msg, e, l, o_msg, o_edge, o_down, o_bil, o_up, sem):
-    move = pltpu.make_async_copy(grad_msg, o_msg, sem)
-    move.start()
-    o_edge[...] = l[:, :D]
-    o_down[...] = l[:, D : D + TW]
-    square = jnp.concatenate([e[:, 128 * j : 128 * j + 128] for j in range(8)], axis=0).T
-    o_bil[...] = square[:B]
-    o_up[0] = e[:, 1024:1088]
-    o_up[1] = e[:, 1088:1152]
-    move.wait()
+def last_kernel(grad_msg, e, l, o_msg, o_edge, o_down, o_bil, o_up):
+    o_msg[...] = grad_msg[...]
+
+    @pl.when(pl.program_id(0) == 0)
+    def _():
+        o_edge[...] = l[:, :D]
+        o_down[...] = l[:, D : D + TW]
+        square = jnp.concatenate([e[:, 128 * j : 128 * j + 128] for j in range(8)], axis=0).T
+        o_bil[...] = square[:B]
+        o_up[0] = e[:, 1024:1088]
+        o_up[1] = e[:, 1088:1152]
 
 
 def last(grad_msg, e, l):
-    vm = pl.BlockSpec(memory_space=pltpu.VMEM)
-    hbm = pl.BlockSpec(memory_space=pl.ANY)
+    whole = lambda shape: pl.BlockSpec(shape, lambda i: (0,) * len(shape))
+    rows = pl.BlockSpec((256, D), lambda i: (i, 0))
     return pl.pallas_call(
         last_kernel,
+        grid=(4,),
         out_shape=[
             jax.ShapeDtypeStruct((E, D), BF),
             jax.ShapeDtypeStruct((16, D), F32),
@@ -572,9 +597,8 @@
             jax.ShapeDtypeStruct((B, 128), F32),
             jax.ShapeDtypeStruct((2, 16, TW), F32),
         ],
-        in_specs=[hbm, vm, vm],
-        out_specs=[hbm, vm, vm, vm, vm],
-        scratch_shapes=[pltpu.SemaphoreType.DMA],
+        in_specs=[rows, whole((16, 1152)), whole((16, 640))],
+        out_specs=[rows, whole((16, D)), whole((16, TW)), whole((B, 128)), whole((2, 16, TW))],
         name="outputs",
     )(grad_msg, e, l)
 
@@ -587,7 +611,7 @@
     narrow = w_down.T
     rows = send_rows[0]
     factor = 1.0 / math.sqrt(lax.axis_size("dp") * lax.axis_size("graph") * E)
-    idx = trip_src[0].reshape(E // G, G, K).transpose(0, 2, 1).reshape(E // G, T)
+    idx = trip_src[0].reshape(E // G, 2, 4, K).transpose(0, 1, 3, 2).reshape(E // G, T)
     outer, bas, state, far = fwd(
         msg, cot, w_edge, narrow, rows, send_count, triplet_basis[0], idx, w_bil
     )

time: 173 us -> 129 us (0.75)
  Pallas kernels: 169 us -> 126 us
    pallas_call x1, Pallas kernels: 34.4 us -> 3.52 us  [last(): pl.pallas_call(last_kernel, grid=(4,), out_shape=[jax.ShapeDtypeStruct((E...]
    pallas_call x1, Pallas kernels: 66.5 us -> 57.7 us  [bwd(): pl.pallas_call(functools.partial(bwd_kernel, factor, n, n_dp), grid=(STEP...]
    pallas_call x1, Pallas kernels: 47.5 us -> 43.7 us  [fwd(): pl.pallas_call(fwd_kernel, grid=(STEPS,), out_shape=[jax.ShapeDtypeStruct...]
where the time goes in v3:
time: 129 us
  Pallas kernels  126 us (98%)
  local copies, waits for them, and re-layouts  2.11 us (2%)
  between operations  1.4 us (1%)
    pallas_call x1, Pallas kernels, bwd(): pl.pallas_call(functools.partial(bwd_kernel, factor, n, n_dp), grid=(STEP...  57.7 us
    pallas_call x1, Pallas kernels, fwd(): pl.pallas_call(fwd_kernel, grid=(STEPS,), out_shape=[jax.ShapeDtypeStruct...  43.7 us
    pallas_call x1, Pallas kernels, mid(): pl.pallas_call(functools.partial(mid_kernel, factor), grid=(E // BE,), ou...  20.7 us
    pallas_call x1, Pallas kernels, last(): pl.pallas_call(last_kernel, grid=(4,), out_shape=[jax.ShapeDtypeStruct((E...  3.52 us

profile of v3, /device:TPU:0, one launch (start us, length us, event | category | flops | bytes accessed | tf_op | source)
XLA Modules:
  0.0 129.2 jit_solution(7192807356163534729)
XLA Ops:
  1.3 1.1 copy.18
  2.4 0.2 copy.19
  2.6 0.8 copy.20.idx
  3.4 43.7 %triplets_out.1 = (bf16[4096,2048]{1,0:T(8,128)(2,1)}, bf16[32768,128]{1,0:T(8,128)(2,1)}, bf16[1024,128]{1,0:T(8,128)(2,1)}, bf16[4,256,512]{2,1,0:T(8,128)(2,1)}) custom-call(bf16[1024,512]{1,0:T(8,128)(2,1)} %bitcast.17, bf16[1024,512]{1,0:T(8,128)(2,1)} %bitcast.13, bf16[512,512]{1,0:T(8,128)(2,1)} %w_edge.3, bf16[64,512]{1,0:T(8,128)(2,1)} %bitcast.22, ...), custom_call_target="tpu_custom_call" | custom-call | tf_op jit(solution)/shard_map/triplets_out/pallas_call | solution.py:222
  47.1 20.7 %middle.1 = (bf16[4096,256]{1,0:T(8,128)(2,1)}, bf16[32,16,1152]{2,1,0:T(8,128)(2,1)}) custom-call(bf16[1024,128]{1,0:T(8,128)(2,1)} %get-tuple-element.19.state, bf16[4096,2048]{1,0:T(8,128)(2,1)} %get-tuple-element.20.outer, bf16[1024,512]{1,0:T(8,128)(2,1)} %bitcast.14, bf16[1024,512]{1,0:T(8,128)(2,1)} %bitcast.15, bf16[1024,512]{1,0:T(8,128)(2,1)} %bitcast.20, ...), custom_call_target="tpu_custom_call" | custom-call | tf_op jit(solution)/shard_map/middle/pallas_call | solution.py:309
  67.8 57.7 %triplets_back.1 = (bf16[1024,512]{1,0:T(8,128)(2,1)}, f32[16,1152]{1,0:T(8,128)}, f32[16,640]{1,0:T(8,128)}) custom-call(bf16[4096,256]{1,0:T(8,128)(2,1)} %get-tuple-element.22.gsx, bf16[32768,128]{1,0:T(8,128)(2,1)} %get-tuple-element.23.bas, s32[128,256]{1,0:T(8,128)} %copy.20.idx, bf16[112,4096]{1,0:T(8,128)(2,1)} %w_bil.3, ...), custom_call_target="tpu_custom_call" | custom-call | tf_op jit(solution)/shard_map/triplets_back/pallas_call | solution.py:530
  125.6 3.5 %outputs.1 = (bf16[1024,512]{1,0:T(8,128)(2,1)}, f32[16,512]{1,0:T(8,128)}, f32[16,64]{1,0:T(8,128)}, f32[112,128]{1,0:T(8,128)}, f32[2,16,64]{2,1,0:T(8,128)}) custom-call(bf16[1024,512]{1,0:T(8,128)(2,1)} %get-tuple-element.25.grad_msg, f32[16,1152]{1,0:T(8,128)} %get-tuple-element.26.e, f32[16,640]{1,0:T(8,128)} %get-tuple-element.27.l), custom_call_target="tpu_custom_call" | custom-call | tf_op jit(solution)/shard_map/outputs/pallas_call | solution.py:590

commit v4 on v3

v4 whole, which is shorter than its diff:
```python
import functools
import math

import jax
import jax.numpy as jnp
from jax import lax
from jax.experimental import pallas as pl
from jax.experimental.pallas import tpu as pltpu
from jax.sharding import PartitionSpec as P

INV_ROOT = 0.7071067811865476
BF = jnp.bfloat16
F32 = jnp.float32
MESH = pl.DeviceIdType.MESH
VMEM_LIMIT = 56 * 1024 * 1024

E = 1024
K = 32
B = 112
TW = 64
D = 512
CAP = 256
NL = 4
G = 8
T = G * K


def offsets(count):
    return [(which // 2 + 1) * (1 - 2 * (which % 2)) for which in range(count)]


def sigmoid(v):
    return 0.5 + 0.5 * jnp.tanh(0.5 * v)


def silu(v):
    return v * sigmoid(v)


def slope(v):
    s = sigmoid(v)
    return s * (1.0 + v * (1.0 - s))


def iota(shape, dim):
    return lax.broadcasted_iota(jnp.int32, shape, dim)


def dot(a, b):
    return jnp.dot(a, b, preferred_element_type=F32)


def dot_nt(a, b):
    return lax.dot_general(a, b, (((1,), (1,)), ((), ())), preferred_element_type=F32)


def dot_tn(a, b):
    return lax.dot_general(a, b, (((0,), (0,)), ((), ())), preferred_element_type=F32)


def onehot(cond):
    return jnp.where(cond, 1.0, 0.0).astype(BF)


GS = 16
GP = 4
STEPS = E // (G * GS)


def graph_at(distance):
    n = lax.axis_size("graph")
    return (lax.axis_index("dp"), lax.rem(lax.axis_index("graph") + (distance + n), n))


def remote(src, dst, send, recv, where):
    return pltpu.make_async_remote_copy(
        src, dst, send, recv, device_id=where, device_id_type=MESH
    )


def greet(where):
    pl.semaphore_signal(
        pltpu.get_barrier_semaphore(), inc=1, device_id=where, device_id_type=MESH
    )


BE = 128
MIDDLE = STEPS
BACK = STEPS + E // BE
ALL = BACK + STEPS
SWAP = BACK + 5


def load_w(wp, w_bil):
    wp[...] = jnp.zeros_like(wp)
    for ch in range(16):
        wp[128 * ch : 128 * ch + B, :] = w_bil[:, 256 * ch : 256 * ch + 256]


def fold(rows):
    half = rows.shape[0] // 2
    return jnp.concatenate([rows[:half], rows[half:]], axis=1)


def unfold(rows):
    return jnp.concatenate([rows[:, :TW], rows[:, TW:]], axis=0)


def kernel(factor, n, n_dp, msg, cot, w_edge, w_down, w_up, rows, rev, count, live, basis, idx, w_bil,
           grad_msg, sum_e, sum_l,
           red, pool_t, wp, sbuf, outer, bas, state, red_send, red_recv, cot_send, cot_recv,
           gsx, bil, up, early, go, acc, ret_send, ret_recv, s_edge, hid, s_down, gedge,
           late, in_e, pair_in, pair_out, in_l, dp_e, dp_l,
           send, recv, e_send, e_recv, l_send, l_recv, r_send, r_recv, p_send, p_recv, d_send, d_recv):
    step = pl.program_id(0)
    shifts = offsets(NL)
    me = lax.axis_index("graph")
    dp = lax.axis_index("dp")
    core = lax.rem(me, 2)
    chip = me // 2
    chips = n // 2

    def red_copy(o):
        where = graph_at(shifts[o])
        return remote(red_send.at[o], red_recv.at[o], send.at[0, o], recv.at[0, o], where)

    def cot_copy(o):
        where = graph_at(shifts[o])
        return remote(cot_send.at[o], cot_recv.at[o], send.at[1, o], recv.at[1, o], where)

    def early_copy(d):
        to = lax.rem(me + d, n)
        return remote(early.at[to], in_e.at[d], e_send.at[d], e_recv.at[d], (dp, to))

    def late_copy(d):
        to = lax.rem(chip + d, chips)
        return remote(pair_out.at[to], in_l.at[d], l_send.at[d], l_recv.at[d], (dp, 2 * to + core))

    def swap(which, buf):
        out = []
        for d in range(1, n_dp):
            where = (lax.rem(dp + d, n_dp), me)
            out.append(remote(buf.at[0], buf.at[d], d_send.at[which, d], d_recv.at[which, d], where))
        return out

    def total(buf):
        terms = [buf[d].astype(F32) for d in range(n_dp)]
        out = jnp.zeros_like(terms[0])
        for source in range(n_dp):
            for d in range(n_dp):
                hit = lax.rem(dp + (n_dp - d), n_dp) == source
                out = out + jnp.where(hit, terms[d], 0.0)
        return out

    @pl.when(step == 0)
    def _():
        def hello(d, carry):
            greet((dp, lax.rem(me + d, n)))
            return carry

        lax.fori_loop(1, n, hello, 0)
        for d in range(1, n_dp):
            greet((lax.rem(dp + d, n_dp), me))
        for i in range(4):
            m = pl.ds(256 * i, 256)
            hidden = silu(dot(msg[m, :], w_edge[...])).astype(BF)
            red[m, :] = silu(dot_nt(hidden, w_down[...])).astype(BF)
        lane = iota((1, CAP), 1)
        lists = []
        for o in range(NL):
            lists.append(jnp.where(lane < count[0, o], rows[o : o + 1, :], -1))
        picks = jnp.concatenate(lists + lists, axis=0).T
        wide = iota((CAP, E), 1)
        for o in range(NL):
            red_send[o] = fold(dot(onehot(wide == picks[:, o : o + 1]), red[...]).astype(BF))
        pl.semaphore_wait(pltpu.get_barrier_semaphore(), n - 1 + n_dp - 1)
        for o in range(NL):
            red_copy(o).start()
        for o in range(NL):
            cot_send[o] = dot(onehot(wide == picks[:, o : o + 1]), cot[...]).astype(BF)
            cot_copy(o).start()
        load_w(wp, w_bil)
        for hi in range(8):
            if hi < 4:
                src = fold(red[256 * hi : 256 * hi + 256, :])
            else:
                red_copy(hi - 4).wait_recv()
                src = red_recv[hi - 4]
            flip = src.astype(F32).T
            pool_t[64 * hi : 64 * hi + 64, :] = jnp.concatenate(
                [flip[:64], flip[64:]], axis=1
            ).astype(BF)

        bil[...] = jnp.zeros_like(bil)
        up[...] = jnp.zeros_like(up)
        acc[...] = jnp.zeros_like(acc)

    @pl.when(step < MIDDLE)
    def _():
        part = step
        keep = onehot(lax.rem(iota((16, T), 1), 4) == iota((16, T), 0) // 4)
        low = iota((8, T), 0) < 4
        low1 = iota((8, 128), 0) < 4

        def some(j, carry):
            hots, his = [], []
            for i in range(GP):
                row = idx[pl.ds(part * GS + j * GP + i, 1), :]
                hots.append(onehot(iota((256, T), 0) == jnp.bitwise_and(row, 255)))
                his.append(jnp.right_shift(row, 8))
            found = dot(pool_t[...], jnp.concatenate(hots, axis=1)).astype(BF)
            founds = [found[:, T * i : T * i + T] for i in range(GP)]
            for i in range(GP):
                g = j * GP + i
                wide = basis[pl.ds(pl.multiple_of(g * G, G), G), :].astype(F32)
                pieces = []
                for k in range(K):
                    piece = wide[:, k * B : (k + 1) * B]
                    pieces.append(jnp.concatenate([piece, jnp.zeros((G, 128 - B), F32)], axis=1))
                first, second = [], []
                for k in range(0, K, 2):
                    x, y = pieces[k], pieces[k + 1]
                    z = pltpu.roll(jnp.where(low1, y, x), 4, 0)
                    first.append(jnp.where(low1, x, z))
                    second.append(jnp.where(low1, z, y))
                first = jnp.concatenate(first, axis=0).astype(BF)
                second = jnp.concatenate(second, axis=0).astype(BF)
                zero = jnp.zeros((128, 128), BF)
                at = pl.multiple_of((part * GS + g) * T, T)
                bas[pl.ds(at, 128), :] = first
                bas[pl.ds(at + 128, 128), :] = second
                rhs = jnp.concatenate(
                    [jnp.concatenate([first, zero], axis=1), jnp.concatenate([zero, second], axis=1)], axis=0
                )
                got = founds[i][:64] * onehot(his[i] == 0)
                for hi in range(1, 8):
                    got = got + founds[i][64 * hi : 64 * hi + 64] * onehot(his[i] == hi)
                got = got.astype(F32)
                tiles = []
                for v in range(8):
                    x = got[8 * v : 8 * v + 8]
                    y = pltpu.roll(x, 4, 0)
                    for d in (jnp.where(low, x, y), jnp.where(low, y, x)):
                        tiles.append(jnp.concatenate([d, d], axis=0).astype(BF) * keep)
                lhs = jnp.concatenate(tiles, axis=0)
                out = dot(lhs, rhs).astype(BF)
                for q in range(2):
                    for ch in range(16):
                        outer[pl.ds(pl.multiple_of((part * GS + g) * 32 + 16 * q, 16), 16), 128 * ch : 128 * ch + 128] = (
                            out[16 * ch : 16 * ch + 16, 128 * q : 128 * q + 128]
                        )
            return carry

        lax.fori_loop(0, GS // GP, some, 0)
        tall = 32 * GS
        full = dot(outer[pl.ds(pl.multiple_of(part * tall, tall), tall), :], wp[...])
        full = jnp.where(lax.rem(iota((tall, 256), 0), 4) == iota((tall, 256), 1) // 64, full, 0.0)
        full = full + pltpu.roll(full, 1, 0)
        full = full + pltpu.roll(full, 2, 0)
        sbuf[...] = full[:, :128] + full[:, 128:]
        picked = sbuf[pl.ds(3, G * GS, stride=4), :]
        state[pl.ds(pl.multiple_of(part * (G * GS), G * GS), G * GS), :] = (picked + pltpu.roll(picked, 64, 1)).astype(BF)

    @pl.when(step == MIDDLE)
    def _():
        for o in range(NL):
            red_copy(o).wait_send()
            cot_copy(o).wait()

    @pl.when((step >= MIDDLE) & (step < BACK))
    def _():
        part = step - MIDDLE
        at = pl.multiple_of(part * BE, BE)
        tall = pl.multiple_of(part * (4 * BE), 4 * BE)
        st = state[pl.ds(at, BE), :][:, :TW]
        alive = iota((BE, D), 0) + at < live[0, 0]
        scaled = jnp.where(alive, cot[pl.ds(at, BE), :].astype(F32) * INV_ROOT, 0.0)
        grad_ca = (scaled * slope(dot(st, w_up[0]))).astype(BF)
        row = rev[pl.ds(part, 1), :]
        col = jnp.concatenate([row] * 8, axis=0).T[:, :1]
        mirror = dot(onehot(iota((BE, E), 1) == col), cot[...])
        mirror = mirror + dot(onehot(iota((BE, NL * CAP), 1) + E == col), cot_recv[...].reshape(NL * CAP, D))
        grad_ac = (mirror * INV_ROOT * slope(dot(st, w_up[1]))).astype(BF)
        up[:TW, :] += dot_tn(st, grad_ca)
        up[TW:, :] += dot_tn(st, grad_ac)
        own = dot_nt(grad_ca, jnp.concatenate([w_up[0]] * 4, axis=0))
        back = dot_nt(grad_ac, jnp.concatenate([w_up[1]] * 4, axis=0)).astype(BF)
        grad_state = (own + back.astype(F32)).astype(BF)
        spread = onehot(iota((4 * BE, BE), 0) // 4 == iota((4 * BE, BE), 1))
        big = dot(spread, grad_state)
        big = jnp.where(lax.rem(iota((4 * BE, 256), 0), 4) == iota((4 * BE, 256), 1) // 64, big, 0.0)
        big = big.astype(BF)
        gsx[pl.ds(tall, 4 * BE), :] = big
        bil[...] += dot_tn(big, outer[pl.ds(tall, 4 * BE), :])

    @pl.when(step == BACK - 1)
    def _():
        turned = (up[...] * factor).T.astype(BF)
        for i in range(32):
            early[i, :, 1024:1152] = turned[16 * i : 16 * i + 16]
            r, c = (i % 2) * 128, (i // 2) * 128
            for j in range(8):
                early[i, :, 128 * j : 128 * j + 128] = (
                    bil[r + 16 * j : r + 16 * j + 16, c : c + 128] * factor
                ).astype(BF)

        def begin(d, carry):
            early_copy(d).start()
            return carry

        lax.fori_loop(1, n, begin, 0)

    @pl.when(step == SWAP)
    def _():
        def take(d, total_):
            early_copy(d).wait()
            return total_ + in_e[d].astype(F32)

        dp_e[0] = lax.fori_loop(1, n, take, early[me].astype(F32)).astype(BF)
        for c in swap(0, dp_e):
            c.start()

    @pl.when(step >= BACK)
    def _():
        part = step - BACK
        go[...] = dot_nt(gsx[pl.ds(pl.multiple_of(part * (32 * GS), 32 * GS), 32 * GS), :], wp[...]).astype(BF)
        e_lane = lax.rem(iota((8, T), 1), 4)
        upper = e_lane >= 2
        odd = lax.rem(e_lane, 2) == 1
        stay = (iota((8, T), 0) >= 4) == odd

        def some(j, carry):
            hots, sides = [], []
            for i in range(GP):
                g = j * GP + i
                row = idx[pl.ds(part * GS + g, 1), :]
                hots.append(onehot(iota((256, T), 0) == jnp.bitwise_and(row, 255)))
                hi_of = jnp.right_shift(row, 8)
                lhs = jnp.concatenate(
                    [
                        jnp.concatenate(
                            [
                                go[pl.ds(pl.multiple_of(g * 32 + 16 * q, 16), 16), 128 * ch : 128 * ch + 128]
                                for q in range(2)
                            ],
                            axis=1,
                        )
                        for ch in range(16)
                    ],
                    axis=0,
                )
                at = pl.multiple_of((part * GS + g) * T, T)
                zero = jnp.zeros((128, 128), BF)
                side = jnp.concatenate(
                    [
                        jnp.concatenate([bas[pl.ds(at, 128), :], zero], axis=1),
                        jnp.concatenate([zero, bas[pl.ds(at + 128, 128), :]], axis=1),
                    ],
                    axis=0,
                )
                full = dot_nt(lhs, side)
                picked = [
                    jnp.where(upper, full[16 * ch + 8 : 16 * ch + 16], full[16 * ch : 16 * ch + 8])
                    for ch in range(16)
                ]
                grads = []
                for v in range(8):
                    z0, z1 = picked[2 * v], picked[2 * v + 1]
                    here = jnp.where(odd, z1, z0)
                    there = jnp.where(odd, z0, z1)
                    grads.append(jnp.where(stay, here, pltpu.roll(there, 4, 0)))
                grad = jnp.concatenate(grads, axis=0).astype(BF)
                sides.append(
                    jnp.concatenate([grad * onehot(hi_of == hi) for hi in range(8)], axis=0)
                )
            acc[...] += dot_nt(jnp.concatenate(sides, axis=1), jnp.concatenate(hots, axis=1))
            return carry

        lax.fori_loop(0, GS // GP, some, 0)

    @pl.when(step == ALL - 1)
    def _():
        def back(o):
            return remote(ret_send.at[o], ret_recv.at[o], r_send.at[o], r_recv.at[o], graph_at(-shifts[o]))

        for o in range(NL):
            part = acc[64 * (4 + o) : 64 * (4 + o) + 64, :]
            ret_send[o] = jnp.concatenate([part[:, :128], part[:, 128:]], axis=0).T.astype(BF)
            back(o).start()
        for i in range(4):
            m = pl.ds(256 * i, 256)
            pre_edge = dot(msg[m, :], w_edge[...])
            s_edge[m, :] = slope(pre_edge)
            hidden = silu(pre_edge).astype(BF)
            hid[m, :] = hidden
            s_down[m, :] = slope(dot_nt(hidden, w_down[...]))
        hots, backs = [], []
        for o in range(NL):
            picks = jnp.where(iota((1, CAP), 1) < count[0, o], rows[o : o + 1, :], -1)
            hots.append(onehot(iota((E, CAP), 0) == picks))
        for o in range(NL):
            back(o).wait()
            backs.append(unfold(ret_recv[o]))
        far = dot(jnp.concatenate(hots, axis=1), jnp.concatenate(backs, axis=0))
        downs = jnp.zeros((D, TW), F32)
        for i in range(4):
            m = pl.ds(256 * i, 256)
            part = acc[64 * i : 64 * i + 64, :]
            own = jnp.concatenate([part[:, :128], part[:, 128:]], axis=0).T
            grad_down = ((far[256 * i : 256 * i + 256] + unfold(own)) * s_down[m, :]).astype(BF)
            downs = downs + dot_tn(hid[m, :], grad_down)
            gedge[m, :] = (dot(grad_down, w_down[...]) * s_edge[m, :]).astype(BF)
        edges = dot_tn(msg[...], gedge[...])
        both = jnp.concatenate(
            [edges * factor, downs * factor, jnp.zeros((D, TW), F32)], axis=1
        ).astype(BF)
        for i in range(n):
            late[i % 2, i // 2] = both[16 * i : 16 * i + 16]
        sibling = (dp, me + 1 - 2 * core)
        first = remote(late.at[1 - core], pair_in, p_send, p_recv, sibling)
        first.start()
        for i in range(4):
            m = pl.ds(256 * i, 256)
            grad_msg[m, :] = dot_nt(gedge[m, :], w_edge[...]).astype(BF)
        first.wait()
        pair_out[...] = (late[core].astype(F32) + pair_in[...].astype(F32)).astype(BF)

        def begin(d, carry):
            late_copy(d).start()
            return carry

        lax.fori_loop(1, chips, begin, 0)
        for c in swap(0, dp_e):
            c.wait()
        sum_e[...] = total(dp_e)

        def take(d, total_):
            late_copy(d).wait()
            return total_ + in_l[d].astype(F32)

        dp_l[0] = lax.fori_loop(1, chips, take, pair_out[chip].astype(F32)).astype(BF)
        for c in swap(1, dp_l):
            c.start()
        for c in swap(1, dp_l):
            c.wait()
        sum_l[...] = total(dp_l)


def run(factor, msg, cot, w_edge, w_down, w_up, rows, rev, count, live, basis, idx, w_bil):
    whole = lambda shape: pl.BlockSpec(
        shape, lambda i: (0,) * len(shape), pipeline_mode=pl.Buffered(1)
    )
    smem = pl.BlockSpec(memory_space=pltpu.SMEM)
    n = lax.axis_size("graph")
    n_dp = lax.axis_size("dp")
    dma = pltpu.SemaphoreType.DMA
    bf = lambda *shape: pltpu.VMEM(shape, BF)
    f32 = lambda *shape: pltpu.VMEM(shape, F32)
    return pl.pallas_call(
        functools.partial(kernel, factor, n, n_dp),
        grid=(ALL,),
        out_shape=[
            jax.ShapeDtypeStruct((E, D), BF),
            jax.ShapeDtypeStruct((16, 1152), F32),
            jax.ShapeDtypeStruct((16, 640), F32),
        ],
        in_specs=[
            whole((E, D)), whole((E, D)), whole((D, D)), whole((TW, D)), whole((2, TW, D)),
            whole((NL, CAP)), whole((8, 128)), smem, smem,
            pl.BlockSpec((G * GS, K * B), lambda i: (jnp.minimum(i, STEPS - 1), 0)),
            whole((E // G, T)), whole((B, 4096)),
        ],
        out_specs=[whole((E, D)), whole((16, 1152)), whole((16, 640))],
        scratch_shapes=[
            bf(E, TW), bf(512, 256), bf(2048, 256), f32(32 * GS, 128),
            bf(4 * E, 2048), bf(E * K, 128), bf(E, 128),
            bf(NL, 128, 128), bf(NL, 128, 128), bf(NL, CAP, D), bf(NL, CAP, D),
            bf(4 * E, 256), f32(256, 2048), f32(2 * TW, D), bf(n, 16, 1152),
            bf(32 * GS, 2048), f32(512, 256), bf(NL, 128, 128), bf(NL, 128, 128),
            f32(E, D), bf(E, D), f32(E, TW), bf(E, D),
            bf(2, n // 2, 16, 640), bf(n, 16, 1152),
            bf(n // 2, 16, 640), bf(n // 2, 16, 640), bf(n // 2, 16, 640),
            bf(n_dp, 16, 1152), bf(n_dp, 16, 640),
            dma((2, NL)), dma((2, NL)), dma((n,)), dma((n,)), dma((n // 2,)), dma((n // 2,)),
            dma((NL,)), dma((NL,)), dma, dma, dma((2, n_dp)), dma((2, n_dp)),
        ],
        compiler_params=pltpu.CompilerParams(
            collective_id=0, has_side_effects=True, vmem_limit_bytes=VMEM_LIMIT
        ),
        name="triplets",
    )(msg, cot, w_edge, w_down, w_up, rows, rev, count, live, basis, idx, w_bil)


def last_kernel(grad_msg, e, l, o_msg, o_edge, o_down, o_bil, o_up):
    o_msg[...] = grad_msg[...]

    @pl.when(pl.program_id(0) == 0)
    def _():
        o_edge[...] = l[:, :D]
        o_down[...] = l[:, D : D + TW]
        square = jnp.concatenate([e[:, 128 * j : 128 * j + 128] for j in range(8)], axis=0).T
        o_bil[...] = square[:B]
        o_up[0] = e[:, 1024:1088]
        o_up[1] = e[:, 1088:1152]


def last(grad_msg, e, l):
    whole = lambda shape: pl.BlockSpec(shape, lambda i: (0,) * len(shape))
    rows = pl.BlockSpec((256, D), lambda i: (i, 0))
    return pl.pallas_call(
        last_kernel,
        grid=(4,),
        out_shape=[
            jax.ShapeDtypeStruct((E, D), BF),
            jax.ShapeDtypeStruct((16, D), F32),
            jax.ShapeDtypeStruct((16, TW), F32),
            jax.ShapeDtypeStruct((B, 128), F32),
            jax.ShapeDtypeStruct((2, 16, TW), F32),
        ],
        in_specs=[rows, whole((16, 1152)), whole((16, 640))],
        out_specs=[rows, whole((16, D)), whole((16, TW)), whole((B, 128)), whole((2, 16, TW))],
        name="outputs",
    )(grad_msg, e, l)


def body(
    messages, cotangent, triplet_basis, w_edge, w_down, w_bil, w_up,
    trip_src, send_rows, send_count, rev_src, edge_count,
):
    factor = 1.0 / math.sqrt(lax.axis_size("dp") * lax.axis_size("graph") * E)
    idx = trip_src[0].reshape(E // G, 2, 4, K).transpose(0, 1, 3, 2).reshape(E // G, T)
    grad_msg, e, l = run(
        factor, messages[0], cotangent[0], w_edge, w_down.T, w_up, send_rows[0],
        rev_src.reshape(8, 128), send_count, edge_count, triplet_basis[0], idx, w_bil,
    )
    grad_msg, g_edge, g_down, g_bil, g_up = last(grad_msg, e, l)
    return grad_msg[None], g_edge, g_down, g_bil, g_up.transpose(0, 2, 1)


def solution(mesh):
    row = P("dp", "graph", None)
    flat = P("dp", "graph")
    return jax.shard_map(
        body,
        mesh=mesh,
        in_specs=(row, row, row, P(), P(), P(), P(), row, row, flat, flat, flat),
        out_specs=(
            row,
            P("graph", None),
            P("graph", None),
            P(None, "graph"),
            P(None, None, "graph"),
        ),
        check_vma=False,
    )
```

time: 129 us -> 119 us (0.922)
  Pallas kernels: 126 us -> 116 us
    pallas_call x3 -> x1, Pallas kernels: 122 us -> 112 us  [run(): pl.pallas_call(functools.partial(kernel, factor, n, n_dp), grid=(ALL,), o...]
where the time goes in v4:
time: 119 us
  Pallas kernels  116 us (97%)
  local copies, waits for them, and re-layouts  2.11 us (2%)
  between operations  1.3 us (1%)
    pallas_call x1, Pallas kernels, run(): pl.pallas_call(functools.partial(kernel, factor, n, n_dp), grid=(ALL,), o...  112 us
    pallas_call x1, Pallas kernels, last(): pl.pallas_call(last_kernel, grid=(4,), out_shape=[jax.ShapeDtypeStruct((E...  3.52 us

profile of v4, /device:TPU:0, one launch (start us, length us, event | category | flops | bytes accessed | tf_op | source)
XLA Modules:
  0.0 119.0 jit_solution(3917861416239158399)
XLA Ops:
  1.3 1.1 copy.18
  2.4 0.2 copy.19
  2.6 0.8 copy.20.idx
  3.4 112.1 %triplets.1 = (bf16[1024,512]{1,0:T(8,128)(2,1)}, f32[16,1152]{1,0:T(8,128)}, f32[16,640]{1,0:T(8,128)}) custom-call(bf16[1024,512]{1,0:T(8,128)(2,1)} %bitcast.14, bf16[1024,512]{1,0:T(8,128)(2,1)} %bitcast.15, bf16[512,512]{1,0:T(8,128)(2,1)} %w_edge.1, bf16[64,512]{1,0:T(8,128)(2,1)} %bitcast.17, bf16[2,64,512]{2,1,0:T(8,128)(2,1)} %w_up.1, ...), custom_call_target="tpu_custom_call" | custom-call | tf_op jit(solution)/shard_map/triplets/pallas_call | solution.py:459
  115.5 3.5 %outputs.1 = (bf16[1024,512]{1,0:T(8,128)(2,1)}, f32[16,512]{1,0:T(8,128)}, f32[16,64]{1,0:T(8,128)}, f32[112,128]{1,0:T(8,128)}, f32[2,16,64]{2,1,0:T(8,128)}) custom-call(bf16[1024,512]{1,0:T(8,128)(2,1)} %get-tuple-element.13.grad_msg, f32[16,1152]{1,0:T(8,128)} %get-tuple-element.14.e, f32[16,640]{1,0:T(8,128)} %get-tuple-element.15.l), custom_call_target="tpu_custom_call" | custom-call | tf_op jit(solution)/shard_map/outputs/pallas_call | solution.py:510

commit v5 on v4

--- a/solution.py
+++ b/solution.py
@@ -63,7 +63,8 @@
 
 
 GS = 16
-GP = 4
+GP = 8
+BP = 16
 STEPS = E // (G * GS)
 
 
@@ -84,7 +85,7 @@
     )
 
 
-BE = 128
+BE = 256
 MIDDLE = STEPS
 BACK = STEPS + E // BE
 ALL = BACK + STEPS
@@ -132,8 +133,7 @@
         to = lax.rem(me + d, n)
         return remote(early.at[to], in_e.at[d], e_send.at[d], e_recv.at[d], (dp, to))
 
-    def late_copy(d):
-        to = lax.rem(chip + d, chips)
+    def late_copy(to, d):
         return remote(pair_out.at[to], in_l.at[d], l_send.at[d], l_recv.at[d], (dp, 2 * to + core))
 
     def swap(which, buf):
@@ -276,8 +276,13 @@
         alive = iota((BE, D), 0) + at < live[0, 0]
         scaled = jnp.where(alive, cot[pl.ds(at, BE), :].astype(F32) * INV_ROOT, 0.0)
         grad_ca = (scaled * slope(dot(st, w_up[0]))).astype(BF)
-        row = rev[pl.ds(part, 1), :]
-        col = jnp.concatenate([row] * 8, axis=0).T[:, :1]
+        col = jnp.concatenate(
+            [
+                jnp.concatenate([rev[pl.ds(part * (BE // 128) + h, 1), :]] * 8, axis=0).T[:, :1]
+                for h in range(BE // 128)
+            ],
+            axis=0,
+        )
         mirror = dot(onehot(iota((BE, E), 1) == col), cot[...])
         mirror = mirror + dot(onehot(iota((BE, NL * CAP), 1) + E == col), cot_recv[...].reshape(NL * CAP, D))
         grad_ac = (mirror * INV_ROOT * slope(dot(st, w_up[1]))).astype(BF)
@@ -324,6 +329,10 @@
     def _():
         part = step - BACK
         go[...] = dot_nt(gsx[pl.ds(pl.multiple_of(part * (32 * GS), 32 * GS), 32 * GS), :], wp[...]).astype(BF)
+
+    @pl.when(step >= BACK)
+    def _():
+        part = step - BACK
         e_lane = lax.rem(iota((8, T), 1), 4)
         upper = e_lane >= 2
         odd = lax.rem(e_lane, 2) == 1
@@ -331,8 +340,8 @@
 
         def some(j, carry):
             hots, sides = [], []
-            for i in range(GP):
-                g = j * GP + i
+            for i in range(BP):
+                g = j * BP + i
                 row = idx[pl.ds(part * GS + g, 1), :]
                 hots.append(onehot(iota((256, T), 0) == jnp.bitwise_and(row, 255)))
                 hi_of = jnp.right_shift(row, 8)
@@ -376,7 +385,7 @@
             acc[...] += dot_nt(jnp.concatenate(sides, axis=1), jnp.concatenate(hots, axis=1))
             return carry
 
-        lax.fori_loop(0, GS // GP, some, 0)
+        lax.fori_loop(0, GS // BP, some, 0)
 
     @pl.when(step == ALL - 1)
     def _():
@@ -410,32 +419,50 @@
             grad_down = ((far[256 * i : 256 * i + 256] + unfold(own)) * s_down[m, :]).astype(BF)
             downs = downs + dot_tn(hid[m, :], grad_down)
             gedge[m, :] = (dot(grad_down, w_down[...]) * s_edge[m, :]).astype(BF)
-        edges = dot_tn(msg[...], gedge[...])
-        both = jnp.concatenate(
-            [edges * factor, downs * factor, jnp.zeros((D, TW), F32)], axis=1
-        ).astype(BF)
-        for i in range(n):
-            late[i % 2, i // 2] = both[16 * i : 16 * i + 16]
         sibling = (dp, me + 1 - 2 * core)
-        first = remote(late.at[1 - core], pair_in, p_send, p_recv, sibling)
-        first.start()
+        quarter = chips // 4
+
+        def pair(j):
+            part = pl.ds(quarter * j, quarter)
+            return remote(late.at[1 - core, part], pair_in.at[part], p_send.at[j], p_recv.at[j], sibling)
+
+        def pass_on(j):
+            pair(j).wait()
+            part = pl.ds(quarter * j, quarter)
+            pair_out[part] = (late[core, part].astype(F32) + pair_in[part].astype(F32)).astype(BF)
+            for i in range(quarter):
+                to = quarter * j + i
+
+                @pl.when(to != chip)
+                def _():
+                    d = lax.rem(to - chip + chips, chips)
+                    late_copy(to, d).start()
+
+        for j in range(4):
+            edges = dot_tn(msg[:, 128 * j : 128 * j + 128], gedge[...])
+            both = jnp.concatenate(
+                [
+                    edges * factor,
+                    downs[128 * j : 128 * j + 128] * factor,
+                    jnp.zeros((128, TW), F32),
+                ],
+                axis=1,
+            ).astype(BF)
+            for i in range(8):
+                late[i % 2, quarter * j + i // 2] = both[16 * i : 16 * i + 16]
+            pair(j).start()
+            if j > 0:
+                pass_on(j - 1)
+        pass_on(3)
         for i in range(4):
             m = pl.ds(256 * i, 256)
             grad_msg[m, :] = dot_nt(gedge[m, :], w_edge[...]).astype(BF)
-        first.wait()
-        pair_out[...] = (late[core].astype(F32) + pair_in[...].astype(F32)).astype(BF)
-
-        def begin(d, carry):
-            late_copy(d).start()
-            return carry
-
-        lax.fori_loop(1, chips, begin, 0)
         for c in swap(0, dp_e):
             c.wait()
         sum_e[...] = total(dp_e)
 
         def take(d, total_):
-            late_copy(d).wait()
+            late_copy(lax.rem(chip + d, chips), d).wait()
             return total_ + in_l[d].astype(F32)
 
         dp_l[0] = lax.fori_loop(1, chips, take, pair_out[chip].astype(F32)).astype(BF)
@@ -482,7 +509,7 @@
             bf(n // 2, 16, 640), bf(n // 2, 16, 640), bf(n // 2, 16, 640),
             bf(n_dp, 16, 1152), bf(n_dp, 16, 640),
             dma((2, NL)), dma((2, NL)), dma((n,)), dma((n,)), dma((n // 2,)), dma((n // 2,)),
-            dma((NL,)), dma((NL,)), dma, dma, dma((2, n_dp)), dma((2, n_dp)),
+            dma((NL,)), dma((NL,)), dma((4,)), dma((4,)), dma((2, n_dp)), dma((2, n_dp)),
         ],
         compiler_params=pltpu.CompilerParams(
             collective_id=0, has_side_effects=True, vmem_limit_bytes=VMEM_LIMIT

time: 119 us -> 112 us (0.941)
  Pallas kernels: 116 us -> 109 us
    pallas_call x1, Pallas kernels: 112 us -> 105 us  [run(): pl.pallas_call(functools.partial(kernel, factor, n, n_dp), grid=(ALL,), o...]
where the time goes in v5:
time: 112 us
  Pallas kernels  109 us (97%)
  local copies, waits for them, and re-layouts  2.11 us (2%)
  between operations  1.3 us (1%)
    pallas_call x1, Pallas kernels, run(): pl.pallas_call(functools.partial(kernel, factor, n, n_dp), grid=(ALL,), o...  105 us
    pallas_call x1, Pallas kernels, last(): pl.pallas_call(last_kernel, grid=(4,), out_shape=[jax.ShapeDtypeStruct((E...  3.52 us

profile of v5, /device:TPU:0, one launch (start us, length us, event | category | flops | bytes accessed | tf_op | source)
XLA Modules:
  0.0 111.9 jit_solution(1049099422637876196)
XLA Ops:
  1.3 1.1 copy.18
  2.4 0.2 copy.19
  2.6 0.8 copy.20.idx
  3.4 105.0 %triplets.1 = (bf16[1024,512]{1,0:T(8,128)(2,1)}, f32[16,1152]{1,0:T(8,128)}, f32[16,640]{1,0:T(8,128)}) custom-call(bf16[1024,512]{1,0:T(8,128)(2,1)} %bitcast.14, bf16[1024,512]{1,0:T(8,128)(2,1)} %bitcast.15, bf16[512,512]{1,0:T(8,128)(2,1)} %w_edge.1, bf16[64,512]{1,0:T(8,128)(2,1)} %bitcast.17, bf16[2,64,512]{2,1,0:T(8,128)(2,1)} %w_up.1, ...), custom_call_target="tpu_custom_call" | custom-call | tf_op jit(solution)/shard_map/triplets/pallas_call | solution.py:486
  108.4 3.5 %outputs.1 = (bf16[1024,512]{1,0:T(8,128)(2,1)}, f32[16,512]{1,0:T(8,128)}, f32[16,64]{1,0:T(8,128)}, f32[112,128]{1,0:T(8,128)}, f32[2,16,64]{2,1,0:T(8,128)}) custom-call(bf16[1024,512]{1,0:T(8,128)(2,1)} %get-tuple-element.13.grad_msg, f32[16,1152]{1,0:T(8,128)} %get-tuple-element.14.e, f32[16,640]{1,0:T(8,128)} %get-tuple-element.15.l), custom_call_target="tpu_custom_call" | custom-call | tf_op jit(solution)/shard_map/outputs/pallas_call | solution.py:537

commit v6 on v5

--- a/solution.py
+++ b/solution.py
@@ -89,7 +89,6 @@
 MIDDLE = STEPS
 BACK = STEPS + E // BE
 ALL = BACK + STEPS
-SWAP = BACK + 5
 
 
 def load_w(wp, w_bil):
@@ -315,16 +314,6 @@
 
         lax.fori_loop(1, n, begin, 0)
 
-    @pl.when(step == SWAP)
-    def _():
-        def take(d, total_):
-            early_copy(d).wait()
-            return total_ + in_e[d].astype(F32)
-
-        dp_e[0] = lax.fori_loop(1, n, take, early[me].astype(F32)).astype(BF)
-        for c in swap(0, dp_e):
-            c.start()
-
     @pl.when(step >= BACK)
     def _():
         part = step - BACK
@@ -457,17 +446,25 @@
         for i in range(4):
             m = pl.ds(256 * i, 256)
             grad_msg[m, :] = dot_nt(gedge[m, :], w_edge[...]).astype(BF)
+
+        def take_early(d, total_):
+            early_copy(d).wait()
+            return total_ + in_e[d].astype(F32)
+
+        dp_e[0] = lax.fori_loop(1, n, take_early, early[me].astype(F32)).astype(BF)
+        for c in swap(0, dp_e):
+            c.start()
+
+        def take(d, total_):
+            late_copy(lax.rem(chip + d, chips), d).wait()
+            return total_ + in_l[d].astype(F32)
+
+        dp_l[0] = lax.fori_loop(1, chips, take, pair_out[chip].astype(F32)).astype(BF)
+        for c in swap(1, dp_l):
+            c.start()
         for c in swap(0, dp_e):
             c.wait()
         sum_e[...] = total(dp_e)
-
-        def take(d, total_):
-            late_copy(lax.rem(chip + d, chips), d).wait()
-            return total_ + in_l[d].astype(F32)
-
-        dp_l[0] = lax.fori_loop(1, chips, take, pair_out[chip].astype(F32)).astype(BF)
-        for c in swap(1, dp_l):
-            c.start()
         for c in swap(1, dp_l):
             c.wait()
         sum_l[...] = total(dp_l)

time: 112 us -> 112 us (level)
  no operation moved by 1% of the time
where the time goes in v6:
time: 112 us; the launch traced here: 111 us
  Pallas kernels  108 us (96%)
  local copies, waits for them, and re-layouts  2.11 us (2%)
  between operations  1.3 us (1%)
    pallas_call x1, Pallas kernels, run(): pl.pallas_call(functools.partial(kernel, factor, n, n_dp), grid=(ALL,), o...  104 us
    pallas_call x1, Pallas kernels, last(): pl.pallas_call(last_kernel, grid=(4,), out_shape=[jax.ShapeDtypeStruct((E...  3.52 us

profile of v6, /device:TPU:0, one launch (start us, length us, event | category | flops | bytes accessed | tf_op | source)
XLA Modules:
  0.0 111.4 jit_solution(17793374166228255985)
XLA Ops:
  1.3 1.1 copy.18
  2.4 0.2 copy.19
  2.6 0.8 copy.20.idx
  3.4 104.5 %triplets.1 = (bf16[1024,512]{1,0:T(8,128)(2,1)}, f32[16,1152]{1,0:T(8,128)}, f32[16,640]{1,0:T(8,128)}) custom-call(bf16[1024,512]{1,0:T(8,128)(2,1)} %bitcast.14, bf16[1024,512]{1,0:T(8,128)(2,1)} %bitcast.15, bf16[512,512]{1,0:T(8,128)(2,1)} %w_edge.1, bf16[64,512]{1,0:T(8,128)(2,1)} %bitcast.17, bf16[2,64,512]{2,1,0:T(8,128)(2,1)} %w_up.1, ...), custom_call_target="tpu_custom_call" | custom-call | tf_op jit(solution)/shard_map/triplets/pallas_call | solution.py:483
  107.9 3.5 %outputs.1 = (bf16[1024,512]{1,0:T(8,128)(2,1)}, f32[16,512]{1,0:T(8,128)}, f32[16,64]{1,0:T(8,128)}, f32[112,128]{1,0:T(8,128)}, f32[2,16,64]{2,1,0:T(8,128)}) custom-call(bf16[1024,512]{1,0:T(8,128)(2,1)} %get-tuple-element.13.grad_msg, f32[16,1152]{1,0:T(8,128)} %get-tuple-element.14.e, f32[16,640]{1,0:T(8,128)} %get-tuple-element.15.l), custom_call_target="tpu_custom_call" | custom-call | tf_op jit(solution)/shard_map/outputs/pallas_call | solution.py:534

commit v7 on v6

--- a/solution.py
+++ b/solution.py
@@ -107,9 +107,9 @@
 
 
 def kernel(factor, n, n_dp, msg, cot, w_edge, w_down, w_up, rows, rev, count, live, basis, idx, w_bil,
-           grad_msg, sum_e, sum_l,
+           gedge, sum_e, sum_l,
            red, pool_t, wp, sbuf, outer, bas, state, red_send, red_recv, cot_send, cot_recv,
-           gsx, bil, up, early, go, acc, ret_send, ret_recv, s_edge, hid, s_down, gedge,
+           gsx, bil, up, early, go, acc, ret_send, ret_recv, s_edge, hid, s_down,
            late, in_e, pair_in, pair_out, in_l, dp_e, dp_l,
            send, recv, e_send, e_recv, l_send, l_recv, r_send, r_recv, p_send, p_recv, d_send, d_recv):
     step = pl.program_id(0)
@@ -443,9 +443,6 @@
             if j > 0:
                 pass_on(j - 1)
         pass_on(3)
-        for i in range(4):
-            m = pl.ds(256 * i, 256)
-            grad_msg[m, :] = dot_nt(gedge[m, :], w_edge[...]).astype(BF)
 
         def take_early(d, total_):
             early_copy(d).wait()
@@ -501,7 +498,7 @@
             bf(NL, 128, 128), bf(NL, 128, 128), bf(NL, CAP, D), bf(NL, CAP, D),
             bf(4 * E, 256), f32(256, 2048), f32(2 * TW, D), bf(n, 16, 1152),
             bf(32 * GS, 2048), f32(512, 256), bf(NL, 128, 128), bf(NL, 128, 128),
-            f32(E, D), bf(E, D), f32(E, TW), bf(E, D),
+            f32(E, D), bf(E, D), f32(E, TW),
             bf(2, n // 2, 16, 640), bf(n, 16, 1152),
             bf(n // 2, 16, 640), bf(n // 2, 16, 640), bf(n // 2, 16, 640),
             bf(n_dp, 16, 1152), bf(n_dp, 16, 640),
@@ -515,8 +512,8 @@
     )(msg, cot, w_edge, w_down, w_up, rows, rev, count, live, basis, idx, w_bil)
 
 
-def last_kernel(grad_msg, e, l, o_msg, o_edge, o_down, o_bil, o_up):
-    o_msg[...] = grad_msg[...]
+def last_kernel(gedge, w_edge, e, l, o_msg, o_edge, o_down, o_bil, o_up):
+    o_msg[...] = dot_nt(gedge[...], w_edge[...]).astype(BF)
 
     @pl.when(pl.program_id(0) == 0)
     def _():
@@ -528,12 +525,12 @@
         o_up[1] = e[:, 1088:1152]
 
 
-def last(grad_msg, e, l):
+def last(gedge, w_edge, e, l):
     whole = lambda shape: pl.BlockSpec(shape, lambda i: (0,) * len(shape))
-    rows = pl.BlockSpec((256, D), lambda i: (i, 0))
+    rows = pl.BlockSpec((512, D), lambda i: (i, 0))
     return pl.pallas_call(
         last_kernel,
-        grid=(4,),
+        grid=(2,),
         out_shape=[
             jax.ShapeDtypeStruct((E, D), BF),
             jax.ShapeDtypeStruct((16, D), F32),
@@ -541,10 +538,10 @@
             jax.ShapeDtypeStruct((B, 128), F32),
             jax.ShapeDtypeStruct((2, 16, TW), F32),
         ],
-        in_specs=[rows, whole((16, 1152)), whole((16, 640))],
+        in_specs=[rows, whole((D, D)), whole((16, 1152)), whole((16, 640))],
         out_specs=[rows, whole((16, D)), whole((16, TW)), whole((B, 128)), whole((2, 16, TW))],
         name="outputs",
-    )(grad_msg, e, l)
+    )(gedge, w_edge, e, l)
 
 
 def body(
@@ -553,11 +550,11 @@
 ):
     factor = 1.0 / math.sqrt(lax.axis_size("dp") * lax.axis_size("graph") * E)
     idx = trip_src[0].reshape(E // G, 2, 4, K).transpose(0, 1, 3, 2).reshape(E // G, T)
-    grad_msg, e, l = run(
+    gedge, e, l = run(
         factor, messages[0], cotangent[0], w_edge, w_down.T, w_up, send_rows[0],
         rev_src.reshape(8, 128), send_count, edge_count, triplet_basis[0], idx, w_bil,
     )
-    grad_msg, g_edge, g_down, g_bil, g_up = last(grad_msg, e, l)
+    grad_msg, g_edge, g_down, g_bil, g_up = last(gedge, w_edge, e, l)
     return grad_msg[None], g_edge, g_down, g_bil, g_up.transpose(0, 2, 1)
 
 

time: 112 us -> 111 us (level)
  no operation moved by 1% of the time
where the time goes in v7:
time: 111 us
  Pallas kernels  108 us (97%)
  local copies, waits for them, and re-layouts  2.11 us (2%)
  between operations  1.3 us (1%)
    pallas_call x1, Pallas kernels, run(): pl.pallas_call(functools.partial(kernel, factor, n, n_dp), grid=(ALL,), o...  104 us
    pallas_call x1, Pallas kernels, last(): pl.pallas_call(last_kernel, grid=(2,), out_shape=[jax.ShapeDtypeStruct((E...  3.11 us

profile of v7, /device:TPU:0, one launch (start us, length us, event | category | flops | bytes accessed | tf_op | source)
XLA Modules:
  0.0 111.0 jit_solution(4633628797234321558)
XLA Ops:
  1.3 1.1 copy.18
  2.4 0.2 copy.19
  2.6 0.8 copy.20.idx
  3.4 104.5 %triplets.1 = (bf16[1024,512]{1,0:T(8,128)(2,1)}, f32[16,1152]{1,0:T(8,128)}, f32[16,640]{1,0:T(8,128)}) custom-call(bf16[1024,512]{1,0:T(8,128)(2,1)} %bitcast.14, bf16[1024,512]{1,0:T(8,128)(2,1)} %bitcast.15, bf16[512,512]{1,0:T(8,128)(2,1)} %w_edge.3, bf16[64,512]{1,0:T(8,128)(2,1)} %bitcast.17, bf16[2,64,512]{2,1,0:T(8,128)(2,1)} %w_up.1, ...), custom_call_target="tpu_custom_call" | custom-call | tf_op jit(solution)/shard_map/triplets/pallas_call | solution.py:480
  107.9 3.1 %outputs.1 = (bf16[1024,512]{1,0:T(8,128)(2,1)}, f32[16,512]{1,0:T(8,128)}, f32[16,64]{1,0:T(8,128)}, f32[112,128]{1,0:T(8,128)}, f32[2,16,64]{2,1,0:T(8,128)}) custom-call(bf16[1024,512]{1,0:T(8,128)(2,1)} %get-tuple-element.13.gedge, bf16[512,512]{1,0:T(8,128)(2,1)} %w_edge.3, f32[16,1152]{1,0:T(8,128)} %get-tuple-element.14.e, f32[16,640]{1,0:T(8,128)} %get-tuple-element.15.l), custom_call_target="tpu_custom_call" | custom-call | tf_op jit(solution)/shard_map/outputs/pallas_call | solution.py:531
